TPU v7x, 32 devices: a whole 2x2x4 slice. The times are simulated.
32 devices in a mesh: batch: 8 (over z, y), tile: 2 (over x), cuts: 2 (over core).
Axes of the slice: x: 2, y: 2, z: 4, core: 2. Of those that a mesh axis runs over, the one named last changes fastest.
Arguments:
- objects: float32 [2, 16, 2, 256, 256], P('cuts', 'tile'), may hold values from -5 to 5
- probe: float32 [4, 2, 256, 256], replicated, may hold values from -5 to 5
- measured: float32 [16, 256, 256], P(('batch', 'tile')), may hold values from 0 to 6
- send_list: int32 [8, 2, 2], P('batch', 'tile'), may hold values from 0 to 7
- corner_slot: int32 [16, 4], P(('batch', 'tile')), may hold values from 0 to 1
- offsets: int32 [16, 2], P(('batch', 'tile')), may hold values from 0 to 255
Outputs:
- new_objects: float32 [2, 16, 2, 256, 256], P('cuts', 'tile')
- new_probe: float32 [4, 2, 256, 256], P('cuts', None, 'tile')
Inputs may be any that keep to these rules, and one draw needn't show every extreme that they name: `send_list`: local tile indices of the owner. `corner_slot`: indices of the owner within the group.
All inputs are finite; a program needn't handle non-finite values.
Results may differ from a plain program's by a relative error of at most 0.0003.
Values sent between devices are 32-bit elements; how exact they have to be, the bound alone decides.
A program may use at most 128 MiB of HBM per device.

v0:
```python
from functools import partial
import math

import jax
import jax.numpy as jnp
from jax import lax
from jax.sharding import PartitionSpec as P

HIGHEST_PRECISION = lax.Precision.HIGHEST
OBJECT_RATE = 0.02
PROBE_RATE = 0.05


def from_behind(block, axis, distance):
    devices = range(lax.axis_size(axis))
    route = [(i - distance, i) for i in devices if i - distance in devices]
    return lax.ppermute(block, axis, route)


def real_product(einsum_form, matrix, field_part):
    return jnp.einsum(einsum_form, matrix, field_part, precision=HIGHEST_PRECISION)


def one_side(matrix, field_pair, einsum_form):
    matrix_re, matrix_im = matrix
    field_re, field_im = field_pair
    return (
        real_product(einsum_form, matrix_re, field_re)
        - real_product(einsum_form, matrix_im, field_im),
        real_product(einsum_form, matrix_re, field_im)
        + real_product(einsum_form, matrix_im, field_re),
    )


def apply_both(matrix, field_pair):
    rows_done = one_side(matrix, field_pair, "jk,...kl->...jl")
    return one_side(matrix, rows_done, "lk,...jk->...jl")


def conjugate(matrix):
    return (matrix[0], -matrix[1])


def complex_times(left_side, right_side):
    return (
        left_side[0] * right_side[0] - left_side[1] * right_side[1],
        left_side[0] * right_side[1] + left_side[1] * right_side[0],
    )


def conj_times(left_side, right_side):
    return (
        left_side[0] * right_side[0] + left_side[1] * right_side[1],
        left_side[0] * right_side[1] - left_side[1] * right_side[0],
    )


def transform_tables(length):
    counter = jnp.arange(length, dtype=jnp.int32)
    turn_index = counter[:, None] * counter[None, :] % length
    angles = 2.0 * math.pi / length * turn_index.astype(jnp.float32)
    wave_re = jnp.cos(angles)
    wave_im = -jnp.sin(angles)
    signed = jnp.where(counter < length // 2, counter, counter - length)
    quadric = signed * signed % (2 * length)
    chirp_angle = math.pi / length * quadric.astype(jnp.float32)
    chirp_re = jnp.cos(chirp_angle)
    chirp_im = -jnp.sin(chirp_angle)
    scaled_re = wave_re * chirp_re[None, :] + wave_im * chirp_im[None, :]
    scaled_im = wave_re * chirp_im[None, :] - wave_im * chirp_re[None, :]
    dot_high = partial(jnp.dot, precision=HIGHEST_PRECISION)
    fresnel = (
        (dot_high(scaled_re, wave_re) - dot_high(scaled_im, wave_im)) / length,
        (dot_high(scaled_re, wave_im) + dot_high(scaled_im, wave_re)) / length,
    )
    unitary = 1.0 / math.sqrt(length)
    return (fresnel, (wave_re * unitary, wave_im * unitary))


def cut_window(region_one, start_cell, length):
    zero_index = jnp.zeros((), jnp.int32)
    return lax.dynamic_slice(
        region_one, (zero_index, start_cell[0], start_cell[1]), (2, length, length)
    )


def place_window(grad_one, start_cell, length):
    zero_index = jnp.zeros((), jnp.int32)
    zero_region = jnp.zeros((2, 2 * length, 2 * length), jnp.float32)
    return lax.dynamic_update_slice(
        zero_region, grad_one, (zero_index, start_cell[0], start_cell[1])
    )


def local(objects, probe, measured, send_list, corner_slot, offsets):
    length = probe.shape[-1]
    mode_count = probe.shape[0]
    half_modes = mode_count // 2
    local_count = measured.shape[0]
    groups = lax.axis_size("tile")
    row_block = length // groups
    slice_index = lax.axis_index("cuts")
    first_slice = slice_index == 0
    fresnel, farfield = transform_tables(length)
    probe_field = (probe[:, 0], probe[:, 1])
    owned_tiles = objects[0]
    pick_list = send_list[0, 0]
    outgoing = jnp.take(owned_tiles, pick_list, axis=0)
    arrived = lax.all_to_all(outgoing, "tile", split_axis=0, concat_axis=0, tiled=True)
    corners = jnp.take(arrived, corner_slot.reshape(-1), axis=0)
    region = corners.reshape(local_count, 2, 2, 2, length, length).transpose(0, 3, 1, 4, 2, 5)
    region = region.reshape(local_count, 2, 2 * length, 2 * length)
    patches = jax.vmap(partial(cut_window, length=length))(region, offsets)

    def forward_part(patch_pair):
        own_patch = (patch_pair[:, 0], patch_pair[:, 1])
        lit_field = complex_times(
            (probe_field[0][None], probe_field[1][None]),
            (own_patch[0][:, None], own_patch[1][:, None]),
        )
        spread = apply_both(fresnel, lit_field)
        return jnp.stack(
            [
                jnp.concatenate([spread[0], own_patch[0][:, None]], axis=1),
                jnp.concatenate([spread[1], own_patch[1][:, None]], axis=1),
            ]
        )

    def middle_part(wave_field, patch_pair, intensity_data):
        spread = (wave_field[0, :, :mode_count], wave_field[1, :, :mode_count])
        earlier = (wave_field[0, :, mode_count][:, None], wave_field[1, :, mode_count][:, None])
        own_patch = (patch_pair[:, 0][:, None], patch_pair[:, 1][:, None])
        exit_wave = complex_times(own_patch, spread)
        far_wave = apply_both(farfield, exit_wave)
        intensity = jnp.sum(far_wave[0] * far_wave[0] + far_wave[1] * far_wave[1], axis=1)
        residual = intensity - intensity_data
        weighted = (residual[:, None] * far_wave[0], residual[:, None] * far_wave[1])
        returned = apply_both(conjugate(farfield), weighted)
        second_terms = conj_times(spread, returned)
        grad_second = jnp.stack(
            [jnp.sum(second_terms[0], axis=1), jnp.sum(second_terms[1], axis=1)], axis=1
        )
        incoming = conj_times(own_patch, returned)
        upper_modes = (incoming[0][:, half_modes:], incoming[1][:, half_modes:])
        spread_back = apply_both(conjugate(fresnel), upper_modes)
        probe_upper = (probe_field[0][None, half_modes:], probe_field[1][None, half_modes:])
        first_terms = conj_times(probe_upper, spread_back)
        part_first = (jnp.sum(first_terms[0], axis=1), jnp.sum(first_terms[1], axis=1))
        probe_terms = conj_times(earlier, spread_back)
        probe_second = jnp.stack(
            [jnp.sum(probe_terms[0], axis=0), jnp.sum(probe_terms[1], axis=0)], axis=1
        )
        back_field = jnp.stack(
            [
                jnp.concatenate([incoming[0][:, :half_modes], part_first[0][:, None]], axis=1),
                jnp.concatenate([incoming[1][:, :half_modes], part_first[1][:, None]], axis=1),
            ]
        )
        return (back_field, grad_second, probe_second)

    def closing_part(back_field, patch_pair):
        lower_modes = (back_field[0, :, :half_modes], back_field[1, :, :half_modes])
        carried = (back_field[0, :, half_modes], back_field[1, :, half_modes])
        own_patch = (patch_pair[:, 0][:, None], patch_pair[:, 1][:, None])
        spread_back = apply_both(conjugate(fresnel), lower_modes)
        probe_lower = (probe_field[0][None, :half_modes], probe_field[1][None, :half_modes])
        first_terms = conj_times(probe_lower, spread_back)
        grad_first = jnp.stack(
            [
                jnp.sum(first_terms[0], axis=1) + carried[0],
                jnp.sum(first_terms[1], axis=1) + carried[1],
            ],
            axis=1,
        )
        probe_terms = conj_times(own_patch, spread_back)
        probe_first = jnp.stack(
            [jnp.sum(probe_terms[0], axis=0), jnp.sum(probe_terms[1], axis=0)], axis=1
        )
        return (grad_first, probe_first)

    def handle(patch_pair, intensity_data):
        position_count = patch_pair.shape[0]
        wave_field = lax.cond(
            first_slice,
            lambda: forward_part(patch_pair),
            lambda: jnp.zeros((2, position_count, mode_count + 1, length, length), jnp.float32),
        )
        wave_field = from_behind(wave_field, "cuts", 1)
        empty_result = lambda: (
            jnp.zeros((2, position_count, half_modes + 1, length, length), jnp.float32),
            jnp.zeros((position_count, 2, length, length), jnp.float32),
            jnp.zeros((half_modes, 2, length, length), jnp.float32),
        )
        back_field, grad_second, probe_second = lax.cond(
            first_slice, empty_result, lambda: middle_part(wave_field, patch_pair, intensity_data)
        )
        back_field = from_behind(back_field, "cuts", -1)
        return lax.cond(
            first_slice,
            lambda: closing_part(back_field, patch_pair),
            lambda: (grad_second, probe_second),
        )

    patch_grads, probe_term = handle(patches, measured)
    region_grads = jax.vmap(partial(place_window, length=length))(patch_grads, offsets)
    corner_grads = region_grads.reshape(local_count, 2, 2, length, 2, length).transpose(
        0, 2, 4, 1, 3, 5
    )
    corner_grads = corner_grads.reshape(local_count * 4, 2, length, length)
    slot_onehot = (
        corner_slot.reshape(-1)[None, :] == jnp.arange(groups, dtype=jnp.int32)[:, None]
    ).astype(jnp.float32)
    slot_grads = jnp.einsum("sk,kcyx->csyx", slot_onehot, corner_grads, precision=HIGHEST_PRECISION)
    probe_blocks = probe_term.reshape(half_modes * 2, groups, row_block, length)
    returned_grads, probe_pieces = (
        lax.all_to_all(slot_grads, "tile", split_axis=1, concat_axis=1, tiled=True),
        lax.all_to_all(probe_blocks, "tile", split_axis=1, concat_axis=1, tiled=True),
    )
    probe_rows = jnp.sum(probe_pieces, axis=1).reshape(half_modes, 2, row_block, length)
    tile_count = owned_tiles.shape[0]
    owner_onehot = (pick_list[None, :] == jnp.arange(tile_count, dtype=jnp.int32)[:, None]).astype(
        jnp.float32
    )
    tile_term = jnp.einsum(
        "ts,csyx->tcyx", owner_onehot, returned_grads, precision=HIGHEST_PRECISION
    )
    tile_total, probe_total = lax.psum((tile_term, probe_rows), "batch")
    new_objects = objects - OBJECT_RATE * tile_total[None]
    zero_index = jnp.zeros((), jnp.int32)
    mode_start = slice_index * half_modes
    row_start = lax.axis_index("tile") * row_block
    own_probe = lax.dynamic_slice(
        probe, (mode_start, zero_index, row_start, zero_index), (half_modes, 2, row_block, length)
    )
    position_total = local_count * lax.axis_size("batch") * groups
    new_probe = own_probe - PROBE_RATE / math.sqrt(position_total) * probe_total
    return (new_objects, new_probe)


def solution(mesh):
    in_specs = (
        P("cuts", "tile", None, None, None),
        P(),
        P(("batch", "tile"), None, None),
        P("batch", "tile", None),
        P(("batch", "tile"), None),
        P(("batch", "tile"), None),
    )
    out_specs = (P("cuts", "tile", None, None, None), P("cuts", None, "tile", None))
    return jax.shard_map(local, mesh=mesh, in_specs=in_specs, out_specs=out_specs, check_vma=False)
```

profile of v0, /device:TPU:24, one launch (start us, length us, event | category | flops | bytes accessed | tf_op | source)
XLA Modules:
  0.0 366.3 jit_solution(3170522718700115921)
XLA Ops:
  8.5 2.8 gather_fusion
  11.3 1.1 broadcast_select_fusion
  12.5 3.6 all-to-all-start
  19.3 1.5 fusion.180
  20.8 1.5 fusion.181
  23.5 1.5 fusion.173
  25.0 1.5 fusion.174
  27.7 3.7 %slice_bitcast_fusion.16 = (f32[4,256,256]{2,1,0:T(8,128)}, f32[4,256,256]{2,1,0:T(8,128)}, f32[4,1,256,256]{3,2,0,1:T(8,128)}, f32[4,1,256,256]{3,2,0,1:T(8,128)}) fusion(f32[4,2,256,256]{3,2,1,0:T(8,128)} %param.15), kind=kLoop, calls=%fused_computation.239 | loop fusion | bytes 6291456 | tf_op jit(solution)/shard_map/squeeze | solution.py:105
  31.4 2.0 gather_fusion.1
  33.4 3.5 fusion.169
  36.9 2.7 reshape.611
  39.6 1.4 constant_dynamic-slice_fusion
  41.0 28.3 %conditional.3 = (f32[2,1,5,256,256]{4,3,2,1,0:T(8,128)}) conditional(s32[]{:T(128)} %convert_element_type.72, () %tuple.39, (f32[4,1,256,256]{3,2,0,1:T(8,128)}, f32[1,2,256,256]{3,2,1,0:T(8,128)S(1)}, f32[4,1,256,256]{3,2,0,1:T(8,128)}, f32[256,256]{1,0:T(8,128)S(1)}, f32[256,256]{1,0:T(8,128)S(1)}) %tuple.40), branch_computations={%region_1.2_spmd, %region_2.3_spmd} | conditional | flops 6447955968 | bytes 54001784 | solution.py:183
  43.5 1.6 copy.184
  45.0 2.0 fusion.12
  47.1 1.1 fusion.2
  48.2 1.8 fusion.10
  50.1 1.1 fusion.16
  51.2 1.1 fusion.3
  52.3 1.9 fusion
  54.2 1.9 fusion.14
  56.1 1.9 fusion.1
  58.2 1.8 pad_maximum_fusion
  69.3 1.5 collective-permute-start
  71.8 3.5 collective-permute-done
  75.3 10.1 %conditional.4 = (f32[2,1,3,256,256]{4,3,2,1,0:T(8,128)S(1)}, f32[1,2,256,256]{3,2,1,0:T(8,128)S(1)}, f32[2,2,256,256]{3,2,0,1:T(8,128)}) conditional(s32[]{:T(128)} %convert_element_type.72, (f32[1,2,256,256]{3,2,1,0:T(8,128)S(1)}, f32[2,1,5,256,256]{4,3,2,1,0:T(8,128)S(1)}, f32[256,256]{1,0:T(8,128)S(1)}, f32[256,256]{1,0:T(8,128)S(1)}, ...), branch_computations={%region_3.9_spmd, %region_9.10_spmd} | conditional | flops 16121987072 | bytes 99614832 | solution.py:194
  85.5 1.6 copy.185
  87.1 1.3 collective-permute-start.1
  89.1 2.7 and_reduce_fusion
  91.8 31.3 %collective-permute-done.1 = f32[2,1,3,256,256]{3,4,2,1,0:T(8,128)S(1)} collective-permute-done((f32[2,1,3,256,256]{3,4,2,1,0:T(8,128)}, f32[2,1,3,256,256]{3,4,2,1,0:T(8,128)S(1)}, u32[]{:S(2)}, u32[]{:S(2)}) %collective-permute-start.1) | collective-permute-done | bytes 1572896 | tf_op jit(solution)/shard_map/ppermute | solution.py:17
  123.1 11.6 %conditional.5 = (f32[2,2,256,256]{3,2,0,1:T(8,128)}, f32[1,2,256,256]{3,2,1,0:T(8,128)S(1)}) conditional(s32[]{:T(128)} %convert_element_type.72, (f32[1,2,256,256]{3,2,1,0:T(8,128)S(1)}, f32[2,2,256,256]{3,2,0,1:T(8,128)}) %tuple.43, (f32[4,256,256]{2,1,0:T(8,128)}, f32[2,1,3,256,256]{3,4,2,1,0:T(8,128)S(1)}, f32[256,256]{1,0:T(8,128)S(1)}, ...), branch_computations={%region_10.11_spmd, %region_11.14_spmd} | conditional | flops 3224240128 | bytes 35127396 | solution.py:198
  128.8 2.1 add_reduce_fusion.2
  130.8 1.6 copy.177
  132.4 1.2 fusion.152
  134.9 1.3 copy.193
  137.2 3.8 %all-to-all-start.2 = ((f32[4,2,128,256]{3,2,0,1:T(8,128)}), f32[4,2,128,256]{3,2,0,1:T(8,128)S(1)}, u32[]{:S(2)}, u32[]{:S(2)}) async-start(f32[4,2,128,256]{3,2,0,1:T(8,128)} %copy.194), calls=%async_computation.2 | async-start | bytes 2097152 | tf_op jit(solution)/shard_map/all_to_all | solution.py:217
  143.0 9.3 %scatter.4 = f32[1,2,512,512]{3,2,1,0:T(8,128)S(1)} dynamic-update-slice(f32[1,2,512,512]{3,2,1,0:T(8,128)S(1)} %broadcast_in_dim.38, f32[1,2,256,256]{3,2,1,0:T(8,128)} %copy.187, s32[]{:T(128)} %constant.119.clone.1, s32[]{:T(128)} %constant.119.clone.1, s32[]{:T(128)} %bitcast.131, s32[]{:T(128)} %bitcast.132) | dynamic-update-slice | bytes 1048580 | tf_op jit(solution)/shard_map/vmap(vmap())/scatter | solution.py:90
  152.3 2.4 reshape.614
  154.6 1.8 copy.188
  156.4 3.2 fusion.170
  159.7 1.1 copy.190
  160.8 3.7 %all-to-all-start.1 = ((f32[2,2,256,256]{3,2,0,1:T(8,128)}), f32[2,2,256,256]{3,2,0,1:T(8,128)S(1)}, u32[]{:S(2)}, u32[]{:S(2)}) async-start(f32[2,2,256,256]{3,2,0,1:T(8,128)} %copy.190), calls=%async_computation.1 | async-start | bytes 2097152 | tf_op jit(solution)/shard_map/all_to_all | solution.py:216
  165.4 8.4 %all-to-all-done.1 = f32[2,2,256,256]{3,2,0,1:T(8,128)S(1)} async-done(((f32[2,2,256,256]{3,2,0,1:T(8,128)}), f32[2,2,256,256]{3,2,0,1:T(8,128)S(1)}, u32[]{:S(2)}, u32[]{:S(2)}) %all-to-all-start.1) | async-done | bytes 1048608 | tf_op jit(solution)/shard_map/all_to_all | solution.py:216
  173.9 4.3 %fusion.175 = f32[8,2,256,256]{3,0,2,1:T(8,128)} fusion(f32[2,2,256,256]{3,2,0,1:T(8,128)S(1)} %all-to-all-done.1, s32[2]{0:T(128)S(1)} %bitcast.397), kind=kOutput, calls=%fused_computation.237 | convolution fusion | flops 25165840 | bytes 5242888 | tf_op jit(solution)/shard_map/ts,csyx->tcyx/dot_general | solution.py:224
  178.2 169.7 %all-reduce.3.cloned.1.call-done = (f32[8,2,256,256]{3,0,2,1:T(8,128)}, f32[2,2,128,256]{3,2,1,0:T(8,128)}) async-done(((f32[8,2,256,256]{3,0,2,1:T(8,128)}, f32[2,2,128,256]{3,2,1,0:T(8,128)}), (f32[8,2,256,256]{3,0,2,1:T(8,128)}, f32[2,2,128,256]{3,2,1,0:T(8,128)})) %all-reduce.3.cloned.1.call-update) | async-done | bytes 4718608 | tf_op jit(solution)/shard_map/psum | solution.py:227
  347.9 6.1 %bitcast_subtract_fusion.1 = f32[1,8,2,256,256]{4,1,3,2,0:T(8,128)S(1)} fusion(f32[1,8,2,256,256]{4,3,2,1,0:T(8,128)} %param.14, f32[8,2,256,256]{3,0,2,1:T(8,128)} %get-tuple-element.221), kind=kLoop, calls=%fused_computation.227 | loop fusion | flops 2097152 | bytes 12582912 | tf_op jit(solution)/shard_map/sub | solution.py:228
  354.1 3.3 copy.195
  357.4 1.9 multiply_subtract_fusion
  (68 shorter events, 19.5 us)
Async XLA Ops:
  11.3 4.7 %copy-start.11 = (s32[1,2]{1,0:T(1,128)S(1)}, s32[1,2]{1,0:T(1,128)}, u32[]{:S(2)}) copy-start(s32[1,2]{1,0:T(1,128)} %param.19) | copy-start | bytes 28
  12.5 18.9 %all-to-all-start = ((f32[2,2,256,256]{3,2,1,0:T(8,128)}), f32[2,2,256,256]{3,2,1,0:T(8,128)S(1)}, u32[]{:S(2)}, u32[]{:S(2)}) async-start(f32[2,2,256,256]{3,2,1,0:T(8,128)} %broadcast_select_fusion), calls=%async_computation | async-start | bytes 2097152 | tf_op jit(solution)/shard_map/all_to_all | solution.py:109
  19.3 2.9 copy-start.14
  41.2 1.9 copy-start.5
  45.0 2.1 copy-start
  56.0 1.9 copy-start.7
  56.0 1.9 copy-start.8
  69.3 6.0 %collective-permute-start = (f32[2,1,5,256,256]{4,3,2,1,0:T(8,128)}, f32[2,1,5,256,256]{4,3,2,1,0:T(8,128)S(1)}, u32[]{:S(2)}, u32[]{:S(2)}) collective-permute-start(f32[2,1,5,256,256]{4,3,2,1,0:T(8,128)} %get-tuple-element.278), channel_id=1, source_target_pairs={{0,1},{2,3},{4,5},{6,7},{8,9},{10,11},{12,13},{14,15},{16,17},{18,... | collective-permute-start | bytes 7864328 | tf_op jit(solution)/shard_map/ppermute | solution.py:17
  85.4 2.9 copy-start.12
  85.5 3.7 %copy-start.13 = (s32[4]{0:T(128)S(1)}, s32[4]{0:T(128)}, u32[]{:S(2)}) copy-start(s32[4]{0:T(128)} %constant.124.clone.1) | copy-start | bytes 52
  87.1 36.0 %collective-permute-start.1 = (f32[2,1,3,256,256]{3,4,2,1,0:T(8,128)}, f32[2,1,3,256,256]{3,4,2,1,0:T(8,128)S(1)}, u32[]{:S(2)}, u32[]{:S(2)}) collective-permute-start(f32[2,1,3,256,256]{3,4,2,1,0:T(8,128)} %copy.185), channel_id=1, source_target_pairs={{1,0},{3,2},{5,4},{7,6},{9,8},{11,10},{13,12},{15,14},{17,16},{19,... | collective-permute-start | bytes 4718600 | tf_op jit(solution)/shard_map/ppermute | solution.py:17
  126.6 2.1 copy-start.2
  126.6 2.1 copy-start.4
  132.4 1.2 copy-start.6
  137.2 23.5 %all-to-all-start.2 = ((f32[4,2,128,256]{3,2,0,1:T(8,128)}), f32[4,2,128,256]{3,2,0,1:T(8,128)S(1)}, u32[]{:S(2)}, u32[]{:S(2)}) async-start(f32[4,2,128,256]{3,2,0,1:T(8,128)} %copy.194), calls=%async_computation.2 | async-start | bytes 2097152 | tf_op jit(solution)/shard_map/all_to_all | solution.py:217
  160.8 13.1 %copy-start.15 = (s32[1,1,2]{2,1,0:T(1,128)S(1)}, s32[1,1,2]{2,1,0:T(1,128)}, u32[]{:S(2)}) copy-start(s32[1,1,2]{2,1,0:T(1,128)} %param.17) | copy-start | bytes 28
  160.8 13.1 %all-to-all-start.1 = ((f32[2,2,256,256]{3,2,0,1:T(8,128)}), f32[2,2,256,256]{3,2,0,1:T(8,128)S(1)}, u32[]{:S(2)}, u32[]{:S(2)}) async-start(f32[2,2,256,256]{3,2,0,1:T(8,128)} %copy.190), calls=%async_computation.1 | async-start | bytes 2097152 | tf_op jit(solution)/shard_map/all_to_all | solution.py:216
  164.5 183.4 %all-reduce.3.cloned.1.call-start = ((), (), s32[]{:S(2)}) async-start(), calls=%async_computation.3 | async-start | bytes 9437184 | tf_op jit(solution)/shard_map/psum | solution.py:227
  354.1 3.3 copy-start.9
Sparse Core Ops, SparseCore 0:
  178.3 169.5 all-reduce.2
where the time goes:
time: 374 us; the launch traced here: 366 us
  waiting for transfers between devices  213 us (57%)
  local copies, waits for them, and re-layouts  44.3 us (12%)
  matrix products  33.8 us (9%)
  other arithmetic  24.4 us (7%)
  loops' own time  18.8 us (5%)
  between operations  18.3 us (5%)
  starting transfers between devices  13.9 us (4%)
    psum x1, waiting for transfers between devices, local(): tile_total, probe_total = lax.psum((tile_term, probe_rows), 'batch')  170 us
    ppermute x2, waiting for transfers between devices, from_behind(): return lax.ppermute(block, axis, route)  34.8 us
    dot_general x16, matrix products, real_product(): jnp.einsum(einsum_form, matrix, field_part, precision=HIGHEST_PRECISION)  20.4 us
    another operation x1, loops' own time, handle(): lax.cond(first_slice, lambda: forward_part(patch_pair), lambda: jnp.zeros...  9.78 us
    scatter x1, local copies, waits for them, and re-layouts, place_window(): lax.dynamic_update_slice(zero_region, grad_one, (zero_index, start_cell[0...  9.31 us
    another operation x1, loops' own time, handle(): lax.cond(first_slice, empty_result, lambda: middle_part(wave_field, patch...  8.89 us
    all_to_all x1, waiting for transfers between devices, local(): lax.all_to_all(slot_grads, 'tile', split_axis=1, concat_axis=1, tiled=True)  8.42 us
  transfers between devices with their start and end apart: 6, of which 4 were waited for; matrix products, arithmetic and copies ran while one was open for 10% of the time, Pallas kernels for 0%

commit v1 on v0

v1 whole, which is shorter than its diff:
```python
import math

import jax
import jax.numpy as jnp
import numpy as np
from jax import lax
from jax.sharding import PartitionSpec as P

HIGH = lax.Precision.HIGH
OBJECT_RATE = 0.02
PROBE_RATE = 0.05


def transform_tables(length):
    counter = np.arange(length)
    wave = np.exp(-2j * np.pi / length * (counter[:, None] * counter[None, :] % length))
    signed = np.where(counter < length // 2, counter, counter - length)
    chirp = np.exp(-1j * np.pi / length * (signed * signed % (2 * length)))
    fresnel = (np.conj(wave) * chirp[None, :]) @ wave / length
    unitary = wave / math.sqrt(length)
    as_pair = lambda m: (np.real(m).astype(np.float32), np.imag(m).astype(np.float32))
    return as_pair(fresnel), as_pair(unitary)


def conjugate(matrix):
    return (matrix[0], -matrix[1])


def complex_times(a, b):
    return (a[0] * b[0] - a[1] * b[1], a[0] * b[1] + a[1] * b[0])


def conj_times(a, b):
    return (a[0] * b[0] + a[1] * b[1], a[0] * b[1] - a[1] * b[0])


def apply_both(matrix, field):
    re, im = matrix
    left = np.concatenate([np.concatenate([re, -im], 1), np.concatenate([im, re], 1)], 0)
    right = np.concatenate([np.concatenate([re, im], 1), np.concatenate([-im, re], 1)], 0)
    length = re.shape[0]
    stacked = jnp.concatenate([field[0], field[1]], axis=-1)
    wide = jnp.einsum("mjk,kl->mjl", stacked, right, precision=HIGH)
    tall = jnp.concatenate([wide[..., :length], wide[..., length:]], axis=-2)
    done = jnp.einsum("jk,mkl->mjl", left, tall, precision=HIGH)
    return (done[:, :length], done[:, length:])


def swap(value, axis):
    return lax.ppermute(value, axis, [(0, 1), (1, 0)])


def local(objects, probe, measured, send_list, corner_slot, offsets):
    length = probe.shape[-1]
    half = probe.shape[0] // 2
    groups = lax.axis_size("tile")
    row_block = length // groups
    cut = lax.axis_index("cuts")
    fresnel, farfield = transform_tables(length)
    owned = objects[0]
    pick = send_list[0, 0]
    outgoing = jnp.take(owned, pick, axis=0)
    arrived = lax.all_to_all(outgoing, "tile", split_axis=0, concat_axis=0, tiled=True)

    y0, x0 = offsets[0, 0], offsets[0, 1]
    cells = jnp.arange(length, dtype=jnp.int32)
    low_row = (cells < y0)[:, None]
    low_col = (cells < x0)[None, :]
    slots = corner_slot[0]
    slot_plane = jnp.where(
        low_row, jnp.where(low_col, slots[3], slots[2]), jnp.where(low_col, slots[1], slots[0])
    )
    tile_own = arrived[0]
    for o in range(1, groups):
        tile_own = jnp.where(slot_plane == o, arrived[o], tile_own)
    tile_other = swap(tile_own, "cuts")
    first = cut == 0
    t0 = jnp.where(first, tile_own, tile_other)
    t1 = jnp.where(first, tile_other, tile_own)
    t0 = (t0[0][None], t0[1][None])
    t1 = (t1[0][None], t1[1][None])
    my_probe = lax.dynamic_slice_in_dim(probe, cut * half, half, 0)
    rolled = jnp.roll(my_probe, (y0, x0), axis=(2, 3))
    p = (rolled[:, 0], rolled[:, 1])

    phi = apply_both(fresnel, complex_times(p, t0))
    psi = apply_both(farfield, complex_times(t1, phi))
    part = jnp.sum(psi[0] * psi[0] + psi[1] * psi[1], axis=0)
    resid = (part + swap(part, "cuts")) - measured[0]
    chi = apply_both(conjugate(farfield), (resid[None] * psi[0], resid[None] * psi[1]))
    g1 = jnp.stack([jnp.sum(v, axis=0) for v in conj_times(phi, chi)])
    zeta = apply_both(conjugate(fresnel), conj_times(t1, chi))
    g0 = jnp.stack([jnp.sum(v, axis=0) for v in conj_times(p, zeta)])
    probe_term = jnp.stack(conj_times(t0, zeta), axis=1)
    probe_term = jnp.roll(probe_term, (-y0, -x0), axis=(2, 3))
    grad = jnp.where(first, g0, g1) + swap(jnp.where(first, g1, g0), "cuts")

    slot_grads = jnp.stack([jnp.where(slot_plane == o, grad, 0.0) for o in range(groups)])
    probe_blocks = probe_term.reshape(half * 2, groups, row_block, length)
    returned = lax.all_to_all(slot_grads, "tile", split_axis=0, concat_axis=0, tiled=True)
    pieces = lax.all_to_all(probe_blocks, "tile", split_axis=1, concat_axis=1, tiled=True)
    probe_rows = jnp.sum(pieces, axis=1).reshape(half, 2, row_block, length)
    tile_count = owned.shape[0]
    tile_ids = jnp.arange(tile_count, dtype=jnp.int32)[:, None, None, None]
    tile_term = jnp.where(pick[0] == tile_ids, returned[0][None], 0.0)
    for s in range(1, groups):
        tile_term = tile_term + jnp.where(pick[s] == tile_ids, returned[s][None], 0.0)
    tile_total, probe_total = lax.psum((tile_term, probe_rows), "batch")
    new_objects = objects - OBJECT_RATE * tile_total[None]
    row_start = lax.axis_index("tile") * row_block
    own_probe = lax.dynamic_slice_in_dim(my_probe, row_start, row_block, 2)
    position_total = lax.axis_size("batch") * groups
    new_probe = own_probe - PROBE_RATE / math.sqrt(position_total) * probe_total
    return (new_objects, new_probe)


def solution(mesh):
    in_specs = (
        P("cuts", "tile", None, None, None),
        P(),
        P(("batch", "tile"), None, None),
        P("batch", "tile", None),
        P(("batch", "tile"), None),
        P(("batch", "tile"), None),
    )
    out_specs = (P("cuts", "tile", None, None, None), P("cuts", None, "tile", None))
    return jax.shard_map(local, mesh=mesh, in_specs=in_specs, out_specs=out_specs, check_vma=False)
```

time: 374 us -> 289 us (0.77)
  local copies, waits for them, and re-layouts: 44.3 us -> 11.1 us
  matrix products: 33.8 us -> 12.2 us
  loops' own time: 18.8 us -> 0 us
  waiting for transfers between devices: 213 us -> 201 us
  other arithmetic: 24.4 us -> 29.1 us
    ppermute x2 -> x3, waiting for transfers between devices: 34.8 us -> 0.01 us  [swap(): return lax.ppermute(value, axis, [(0, 1), (1, 0)])]
    dot_general x22 -> x8, matrix products: 33.8 us -> 12.2 us  [the longest x4 6.61 us: apply_both(): done = jnp.einsum('jk,mkl->mjl', left, tall, precision=HIGH)]
    another operation x3 -> x0, loops' own time: 18.8 us -> none  [the longest x1 9.78 us: handle(): lax.cond(first_slice, lambda: forward_part(patch_pair), lambda: jnp.zeros...]
    all_to_all x1, waiting for transfers between devices: 0.01 us -> 13.2 us  [local(): lax.all_to_all(probe_blocks, 'tile', split_axis=1, concat_axis=1, tiled=T...]
    scatter x1 -> x0, local copies, waits for them, and re-layouts: 9.31 us -> none  [place_window(): lax.dynamic_update_slice(zero_region, grad_one, (zero_index, start_cell[0...]
    all_to_all x1, waiting for transfers between devices: 0.01 us -> 8.67 us  [local(): lax.all_to_all(outgoing, 'tile', split_axis=0, concat_axis=0, tiled=True)]
    another operation x9 -> x0, local copies, waits for them, and re-layouts: 6.58 us -> none
    select_n x3 -> x6, other arithmetic: 1.81 us -> 7.87 us  [the longest x1 3.09 us: local(): jnp.where(low_col, slots[1], slots[0])]
  transfers between devices with their start and end apart: 6 -> 7, of which waited for: 4 -> 4; matrix products, arithmetic and copies ran while one was open for 10% -> 5% of each run, Pallas kernels for 0% -> 0%
where the time goes in v1:
time: 289 us; the launch traced here: 284 us
  waiting for transfers between devices  201 us (70%)
  other arithmetic  29.1 us (10%)
  between operations  19.8 us (7%)
  matrix products  12.2 us (4%)
  starting transfers between devices  11.4 us (4%)
  local copies, waits for them, and re-layouts  11.1 us (4%)
    psum x1, waiting for transfers between devices, local(): tile_total, probe_total = lax.psum((tile_term, probe_rows), 'batch')  168 us
    all_to_all x1, waiting for transfers between devices, local(): lax.all_to_all(probe_blocks, 'tile', split_axis=1, concat_axis=1, tiled=T...  13.2 us
    all_to_all x1, waiting for transfers between devices, local(): lax.all_to_all(slot_grads, 'tile', split_axis=0, concat_axis=0, tiled=True)  10.9 us
    all_to_all x1, waiting for transfers between devices, local(): lax.all_to_all(outgoing, 'tile', split_axis=0, concat_axis=0, tiled=True)  8.67 us
    dot_general x4, matrix products, apply_both(): done = jnp.einsum('jk,mkl->mjl', left, tall, precision=HIGH)  6.61 us
    sub x1, other arithmetic, local(): new_objects = objects - OBJECT_RATE * tile_total[None]  6.14 us
  transfers between devices with their start and end apart: 7, of which 4 were waited for; matrix products, arithmetic and copies ran while one was open for 5% of the time, Pallas kernels for 0%

profile of v1, /device:TPU:24, one launch (start us, length us, event | category | flops | bytes accessed | tf_op | source)
XLA Modules:
  0.0 284.4 jit_solution(10464383342744031404)
XLA Ops:
  7.2 0.8 compare_and_fusion
  8.0 0.7 fusion.38
  8.7 2.8 gather_fusion
  11.5 1.1 broadcast_select_fusion
  12.6 3.6 %all-to-all-start = ((f32[2,2,256,256]{3,2,1,0:T(8,128)}), f32[2,2,256,256]{3,2,1,0:T(8,128)S(1)}, u32[]{:S(2)}, u32[]{:S(2)}) async-start(f32[2,2,256,256]{3,2,1,0:T(8,128)} %broadcast_select_fusion), calls=%async_computation | async-start | bytes 2097152 | tf_op jit(solution)/shard_map/all_to_all | solution.py:63
  16.2 0.6 fusion.52
  16.8 0.6 iota_compare_fusion.1
  17.5 0.7 fusion.53
  18.1 3.1 %fusion.36 = (s32[256]{0:T(256)S(1)}, s32[256]{0:T(256)S(1)}) fusion(s32[]{:T(128)} %bitcast.6, s32[]{:T(128)} %bitcast.5, s32[]{:T(128)} %bitcast.2, s32[]{:T(128)} %bitcast.4, s32[]{:T(128)} %bitcast.3), kind=kLoop, calls=%fused_computation.97 | loop fusion | flops 768 | bytes 2068 | tf_op jit(solution)/shard_map/jit(_where)/select_n | solution.py:71
  21.2 0.2 select_compare_fusion
  21.4 8.7 %all-to-all-done = f32[2,2,256,256]{3,2,1,0:T(8,128)S(1)} async-done(((f32[2,2,256,256]{3,2,1,0:T(8,128)}), f32[2,2,256,256]{3,2,1,0:T(8,128)S(1)}, u32[]{:S(2)}, u32[]{:S(2)}) %all-to-all-start) | async-done | bytes 1048608 | tf_op jit(solution)/shard_map/all_to_all | solution.py:63
  30.1 0.9 fusion.34
  34.9 1.1 fusion.4
  36.0 2.1 broadcast_select_fusion.2
  38.2 0.8 copy.60
  39.0 1.1 slice_bitcast_fusion.8
  40.3 0.5 copy-done.9
  40.9 1.0 fusion.6
  42.1 1.9 convolution_bitcast_fusion.3
  44.1 1.0 fusion.13
  45.2 1.9 convolution_bitcast_fusion.2
  47.1 0.8 add_reduce_fusion.2
  47.9 0.5 collective-permute-start.1
  48.4 1.8 copy.63
  50.2 1.2 bitcast_subtract_fusion.1
  51.6 2.3 fusion.20
  54.0 1.9 convolution_bitcast_fusion.1
  55.9 1.0 multiply_add_fusion
  56.9 1.3 fusion.27
  58.3 1.0 convolution_bitcast_fusion
  59.3 0.3 subtract_bitcast_fusion
  59.9 0.1 collective-permute-start.2
  61.4 0.3 fusion.2
  61.7 0.6 fusion
  62.4 1.0 copy.72
  63.5 3.6 %all-to-all-start.2 = ((f32[4,2,128,256]{3,2,0,1:T(8,128)}), f32[4,2,128,256]{3,2,0,1:T(8,128)S(1)}, u32[]{:S(2)}, u32[]{:S(2)}) async-start(f32[4,2,128,256]{3,2,0,1:T(8,128)} %copy.72), calls=%async_computation.2 | async-start | bytes 2097152 | tf_op jit(solution)/shard_map/all_to_all | solution.py:101
  67.1 0.1 select_bitcast_fusion.1
  67.3 1.0 pad_maximum_fusion
  68.3 13.2 %all-to-all-done.2 = f32[4,2,128,256]{3,2,0,1:T(8,128)S(1)} async-done(((f32[4,2,128,256]{3,2,0,1:T(8,128)}), f32[4,2,128,256]{3,2,0,1:T(8,128)S(1)}, u32[]{:S(2)}, u32[]{:S(2)}) %all-to-all-start.2) | async-done | bytes 1048608 | tf_op jit(solution)/shard_map/all_to_all | solution.py:101
  81.5 3.6 %all-to-all-start.1 = ((f32[2,2,256,256]{3,2,1,0:T(8,128)}), f32[2,2,256,256]{3,2,1,0:T(8,128)S(1)}, u32[]{:S(2)}, u32[]{:S(2)}) async-start(f32[2,2,256,256]{3,2,1,0:T(8,128)} %pad_maximum_fusion), calls=%async_computation.1 | async-start | bytes 2097152 | tf_op jit(solution)/shard_map/all_to_all | solution.py:100
  85.2 0.6 fusion.51
  85.7 1.2 iota_compare_fusion.2
  87.0 0.9 reduce_sum.59
  87.9 10.9 %all-to-all-done.1 = f32[2,2,256,256]{3,2,1,0:T(8,128)S(1)} async-done(((f32[2,2,256,256]{3,2,1,0:T(8,128)}), f32[2,2,256,256]{3,2,1,0:T(8,128)S(1)}, u32[]{:S(2)}, u32[]{:S(2)}) %all-to-all-start.1) | async-done | bytes 1048608 | tf_op jit(solution)/shard_map/all_to_all | solution.py:100
  98.9 2.6 select_add_fusion
  101.5 167.9 %all-reduce.3.cloned.1.call-done = (f32[8,2,256,256]{3,2,1,0:T(8,128)}, f32[2,2,128,256]{3,2,1,0:T(8,128)}) async-done(((f32[8,2,256,256]{3,2,1,0:T(8,128)}, f32[2,2,128,256]{3,2,1,0:T(8,128)}), (f32[8,2,256,256]{3,2,1,0:T(8,128)}, f32[2,2,128,256]{3,2,1,0:T(8,128)})) %all-reduce.3.cloned.1.call-update) | async-done | bytes 4718608 | tf_op jit(solution)/shard_map/psum | solution.py:108
  269.4 6.1 %bitcast_subtract_fusion = f32[1,8,2,256,256]{4,3,2,1,0:T(8,128)} fusion(f32[1,8,2,256,256]{4,3,2,1,0:T(8,128)} %param.16, f32[8,2,256,256]{3,2,1,0:T(8,128)} %get-tuple-element.7), kind=kLoop, calls=%fused_computation.1 | loop fusion | flops 2097152 | bytes 12582912 | tf_op jit(solution)/shard_map/sub | solution.py:109
  275.6 2.0 multiply_subtract_fusion
  (60 shorter events, 1.8 us)
Async XLA Ops:
  7.2 9.0 %copy-start.17 = (s32[1,2]{1,0:T(1,128)S(1)}, s32[1,2]{1,0:T(1,128)}, u32[]{:S(2)}) copy-start(s32[1,2]{1,0:T(1,128)} %param.21) | copy-start | bytes 28
  7.2 10.3 %copy-start.16 = (s32[1,4]{1,0:T(1,128)S(1)}, s32[1,4]{1,0:T(1,128)}, u32[]{:S(2)}) copy-start(s32[1,4]{1,0:T(1,128)} %param.20) | copy-start | bytes 52
  7.2 27.6 %copy-start.13 = (f32[4,2,256,256]{3,2,1,0:T(8,128)S(1)}, f32[4,2,256,256]{3,2,1,0:T(8,128)}, u32[]{:S(2)}) copy-start(f32[4,2,256,256]{3,2,1,0:T(8,128)} %param.17) | copy-start | bytes 6291460
  12.6 17.4 %all-to-all-start = ((f32[2,2,256,256]{3,2,1,0:T(8,128)}), f32[2,2,256,256]{3,2,1,0:T(8,128)S(1)}, u32[]{:S(2)}, u32[]{:S(2)}) async-start(f32[2,2,256,256]{3,2,1,0:T(8,128)} %broadcast_select_fusion), calls=%async_computation | async-start | bytes 2097152 | tf_op jit(solution)/shard_map/all_to_all | solution.py:63
  30.9 5.1 %collective-permute-start = (f32[2,256,256]{2,1,0:T(8,128)}, f32[2,256,256]{2,1,0:T(8,128)}, u32[]{:S(2)}, u32[]{:S(2)}) collective-permute-start(f32[2,256,256]{2,1,0:T(8,128)} %fusion.34), channel_id=1, source_target_pairs={{0,1},{1,0},{2,3},{3,2},{4,5},{5,4},{6,7},{7,6},{8,9},{9,8},{10,11... | collective-permute-start | bytes 1572872 | tf_op jit(solution)/shard_map/ppermute | solution.py:50
  36.0 5.0 %copy-start = (f32[512,512,1]{1,0,2:T(8,128)S(1)}, f32[512,512,1]{1,0,2:T(8,128)}, u32[]{:S(2)}) copy-start(f32[512,512,1]{1,0,2:T(8,128)} %constant.98) | copy-start | bytes 3145732
  40.1 0.7 copy-start.9
  40.1 0.8 copy-start.11
  40.1 1.9 copy-start.2
  40.9 3.0 %copy-start.7 = (f32[256,256]{0,1:T(8,128)S(1)}, f32[256,256]{0,1:T(8,128)}, u32[]{:S(2)}) copy-start(f32[256,256]{0,1:T(8,128)} %copy.60) | copy-start | bytes 786436
  41.9 2.1 copy-start.4
  43.9 1.3 copy-start.6
  47.9 2.3 collective-permute-start.1
  50.2 3.8 %copy-start.5 = (f32[512,512,1]{1,0,2:T(8,128)S(1)}, f32[512,512,1]{1,0,2:T(8,128)}, u32[]{:S(2)}) copy-start(f32[512,512,1]{1,0,2:T(8,128)} %constant.100) | copy-start | bytes 3145732
  51.6 4.3 %copy-start.8 = (f32[256,256]{0,1:T(8,128)S(1)}, f32[256,256]{0,1:T(8,128)}, u32[]{:S(2)}) copy-start(f32[256,256]{0,1:T(8,128)} %copy.60) | copy-start | bytes 786436
  54.0 2.9 %copy-start.3 = (f32[512,512,1]{1,0,2:T(8,128)S(1)}, f32[512,512,1]{1,0,2:T(8,128)}, u32[]{:S(2)}) copy-start(f32[512,512,1]{1,0,2:T(8,128)} %constant.99) | copy-start | bytes 3145732
  55.9 2.4 copy-start.1
  56.9 2.4 copy-start.10
  56.9 2.4 copy-start.12
  58.2 1.4 copy-start.14
  59.9 7.1 %collective-permute-start.2 = (f32[2,256,256]{2,1,0:T(8,128)S(1)}, f32[2,256,256]{2,1,0:T(8,128)S(1)}, u32[]{:S(2)}, u32[]{:S(2)}) collective-permute-start(f32[2,256,256]{2,1,0:T(8,128)S(1)} %fusion.35), channel_id=1, source_target_pairs={{0,1},{1,0},{2,3},{3,2},{4,5},{5,4},{6,7},{7,6},{8,9},{9,8},{10,11... | collective-permute-start | bytes 1572872 | tf_op jit(solution)/shard_map/ppermute | solution.py:50
  63.5 18.1 %all-to-all-start.2 = ((f32[4,2,128,256]{3,2,0,1:T(8,128)}), f32[4,2,128,256]{3,2,0,1:T(8,128)S(1)}, u32[]{:S(2)}, u32[]{:S(2)}) async-start(f32[4,2,128,256]{3,2,0,1:T(8,128)} %copy.72), calls=%async_computation.2 | async-start | bytes 2097152 | tf_op jit(solution)/shard_map/all_to_all | solution.py:101
  67.0 18.1 %copy-start.18 = (s32[1,1,2]{2,1,0:T(1,128)S(1)}, s32[1,1,2]{2,1,0:T(1,128)}, u32[]{:S(2)}) copy-start(s32[1,1,2]{2,1,0:T(1,128)} %param.19) | copy-start | bytes 28
  81.5 17.3 %all-to-all-start.1 = ((f32[2,2,256,256]{3,2,1,0:T(8,128)}), f32[2,2,256,256]{3,2,1,0:T(8,128)S(1)}, u32[]{:S(2)}, u32[]{:S(2)}) async-start(f32[2,2,256,256]{3,2,1,0:T(8,128)} %pad_maximum_fusion), calls=%async_computation.1 | async-start | bytes 2097152 | tf_op jit(solution)/shard_map/all_to_all | solution.py:100
  85.1 184.3 %all-reduce.3.cloned.1.call-start = ((), (), s32[]{:S(2)}) async-start(), calls=%async_computation.3 | async-start | bytes 9437184 | tf_op jit(solution)/shard_map/psum | solution.py:108
  269.4 6.1 %copy-start.15 = (f32[2,2,128,256]{3,2,1,0:T(8,128)S(1)}, f32[2,2,128,256]{3,2,1,0:T(8,128)}, u32[]{:S(2)}) copy-start(f32[2,2,128,256]{3,2,1,0:T(8,128)} %get-tuple-element.8) | copy-start | bytes 1572868
Sparse Core Ops, SparseCore 0:
  101.6 167.7 all-reduce.2

commit v2 on v1

--- a/solution.py
+++ b/solution.py
@@ -1,12 +1,15 @@
+import functools
 import math
 
 import jax
 import jax.numpy as jnp
 import numpy as np
 from jax import lax
+from jax.experimental import pallas as pl
+from jax.experimental.pallas import tpu as pltpu
 from jax.sharding import PartitionSpec as P
 
-HIGH = lax.Precision.HIGH
+EXACT = lax.Precision.HIGHEST
 OBJECT_RATE = 0.02
 PROBE_RATE = 0.05
 
@@ -40,20 +43,209 @@
     right = np.concatenate([np.concatenate([re, im], 1), np.concatenate([-im, re], 1)], 0)
     length = re.shape[0]
     stacked = jnp.concatenate([field[0], field[1]], axis=-1)
-    wide = jnp.einsum("mjk,kl->mjl", stacked, right, precision=HIGH)
+    wide = jnp.einsum("mjk,kl->mjl", stacked, right, precision=EXACT)
     tall = jnp.concatenate([wide[..., :length], wide[..., length:]], axis=-2)
-    done = jnp.einsum("jk,mkl->mjl", left, tall, precision=HIGH)
+    done = jnp.einsum("jk,mkl->mjl", left, tall, precision=EXACT)
     return (done[:, :length], done[:, length:])
 
 
 def swap(value, axis):
     return lax.ppermute(value, axis, [(0, 1), (1, 0)])
+
+
+MESH = pl.DeviceIdType.MESH
+
+
+def reduce_kernel(
+    batches, groups, rows, chunks,
+    msg, prb, own_obj, own_prb, out_obj, out_prb,
+    got, px, ps, py, obj, prn,
+    g_send, g_recv, f_send, f_recv, x_send, x_recv, y_send, y_recv,
+    a_send, a_recv, b_send, b_recv, l_sem,
+):
+    me, mine = lax.axis_index("batch"), lax.axis_index("tile")
+    depth = batches // 2
+    pair = me + 1 - 2 * (me % 2)
+    tiles = own_obj.shape[0] // 2
+    behind = lambda d: (me + batches - d) % batches
+
+    barrier = pltpu.get_barrier_semaphore()
+    for d in range(1, batches):
+        pl.semaphore_signal(
+            barrier, inc=1, device_id={"batch": (me + d) % batches}, device_id_type=MESH
+        )
+    for e in range(1, groups):
+        pl.semaphore_signal(
+            barrier, inc=1, device_id={"tile": (mine + e) % groups}, device_id_type=MESH
+        )
+    pl.semaphore_wait(barrier, batches + groups - 2)
+
+    def send(src, dst, sems, place, target):
+        copy = pltpu.make_async_remote_copy(
+            src_ref=src, dst_ref=dst, send_sem=sems[0].at[place], recv_sem=sems[1].at[place],
+            device_id=target, device_id_type=MESH,
+        )
+        copy.start()
+        return copy
+
+    to_batch = lambda d: {"batch": (me + d) % batches}
+    to_tile = lambda e: {"tile": (mine + e) % groups}
+    sent = []
+    first = {}
+    halves = []
+    for e in range(1, groups):
+        halves.append(
+            send(prb.at[(mine + e) % groups], px.at[e], (x_send, x_recv), e, to_tile(e))
+        )
+    for d in range(1, batches):
+        first[d] = send(
+            msg.at[(me + d) % batches], got.at[0, d], (g_send, g_recv), d, to_batch(d)
+        )
+    got[0, 0] = msg[me]
+    forwards = []
+
+    def forward(d):
+        for e in range(1, groups):
+            forwards.append(
+                send(got.at[0, d], got.at[e, d], (f_send, f_recv), e * batches + d, to_tile(e))
+            )
+
+    forward(0)
+    for copy in halves:
+        copy.wait()
+
+    def add_probe(b, carry):
+        total = prb[mine, b]
+        for e in range(1, groups):
+            total = total + px[e, b]
+        ps[b] = total
+        return carry
+
+    lax.fori_loop(0, batches, add_probe, 0)
+    probe_sends = [
+        send(ps.at[(me + d) % batches], py.at[d], (y_send, y_recv), d, to_batch(d))
+        for d in range(1, batches)
+    ]
+    for d in range(1, batches):
+        first[d].wait_recv()
+        forward(d)
+    for copy in forwards:
+        copy.wait()
+
+    mine_f = mine.astype(jnp.float32)
+    strips = rows // 8
+
+    def add_strip(i, carry):
+        plane, strip = i // strips, i % strips
+        start = pl.multiple_of(i * 8, 8)
+        row = (lax.broadcasted_iota(jnp.int32, (8, 256), 0) + strip * 8).astype(jnp.float32)
+        sums = [jnp.zeros((8, 256), jnp.float32) for _ in range(tiles)]
+        for d in range(batches):
+            for e in range(groups):
+                upper = got[e, d, pl.ds(2 * rows, 1), :]
+                lower = got[e, d, pl.ds(2 * rows + 1, 1), :]
+                edge = got[e, d, pl.ds(2 * rows + 2, 1), :]
+                place = got[0, d, pl.ds(2 * rows + 3 + e, 1), :]
+                slot = jnp.where(row < edge, lower, upper)
+                value = jnp.where(slot == mine_f, got[e, d, pl.ds(start, 8), :], 0.0)
+                for j in range(tiles):
+                    sums[j] = sums[j] + jnp.where(place == float(j), value, 0.0)
+        spot = pl.multiple_of(strip * 8, 8)
+        for j in range(tiles):
+            obj[2 * j + plane, pl.ds(spot, 8), :] = (
+                own_obj[2 * j + plane, pl.ds(spot, 8), :] - OBJECT_RATE * sums[j]
+            )
+        return carry
+
+    lax.fori_loop(0, 2 * strips, add_strip, 0)
+
+    locals_ = [pltpu.make_async_copy(obj, out_obj.at[:, me], l_sem.at[0])]
+    locals_[0].start()
+    part = 2 * tiles // chunks
+    pieces = [pl.ds(q * part, part) for q in range(chunks)]
+    arriving = {}
+
+    def gather_start(q, src, dst):
+        base = q * depth
+        arriving[q, 0] = send(src, dst, (a_send, a_recv), base, {"batch": pair})
+        for k in range(1, depth):
+            arriving[q, k] = send(src, dst, (a_send, a_recv), base + k, to_batch(2 * k))
+
+    for q in range(chunks):
+        gather_start(q, obj.at[pieces[q]], out_obj.at[pieces[q], me])
+
+    for copy in probe_sends:
+        copy.wait()
+    total = ps[me]
+    for d in range(1, batches):
+        total = total + py[d]
+    prn[...] = own_prb[...] - PROBE_RATE / math.sqrt(batches * groups) * total
+    locals_.append(pltpu.make_async_copy(prn, out_prb.at[me], l_sem.at[1]))
+    locals_[1].start()
+    gather_start(chunks, prn, out_prb.at[me])
+
+    relays = []
+    for q in range(chunks + 1):
+        for k in range(1, depth):
+            arriving[q, k].wait_recv()
+            b = behind(2 * k)
+            ref = out_obj.at[pieces[q], b] if q < chunks else out_prb.at[b]
+            relays.append(send(ref, ref, (b_send, b_recv), q * depth + k, {"batch": pair}))
+    for q in range(chunks + 1):
+        arriving[q, 0].wait_recv()
+    for copy in relays:
+        copy.wait()
+    for copy in arriving.values():
+        copy.wait_send()
+    for d in range(1, batches):
+        first[d].wait_send()
+    for copy in locals_:
+        copy.wait()
+
+
+def reduce_and_gather(messages, probe_blocks, own_objects, own_probe, batches, groups, rows):
+    length = messages.shape[-1]
+    chunks = 4
+    depth = batches // 2
+    dma = pltpu.SemaphoreType.DMA
+    f32 = jnp.float32
+    probe_rows = own_probe.shape[0]
+    vmem = pl.BlockSpec(memory_space=pltpu.VMEM)
+    return pl.pallas_call(
+        functools.partial(reduce_kernel, batches, groups, rows, chunks),
+        out_shape=(
+            jax.ShapeDtypeStruct((own_objects.shape[0], batches, rows, length), f32),
+            jax.ShapeDtypeStruct((batches, probe_rows, length), f32),
+        ),
+        in_specs=[vmem] * 4,
+        out_specs=(pl.BlockSpec(memory_space=pl.ANY), pl.BlockSpec(memory_space=pl.ANY)),
+        scratch_shapes=[
+            pltpu.VMEM((groups, batches) + messages.shape[1:], f32),
+            pltpu.VMEM((groups, batches, probe_rows, length), f32),
+            pltpu.VMEM((batches, probe_rows, length), f32),
+            pltpu.VMEM((batches, probe_rows, length), f32),
+            pltpu.VMEM(own_objects.shape, f32),
+            pltpu.VMEM(own_probe.shape, f32),
+            dma((batches,)), dma((batches,)),
+            dma((groups * batches,)), dma((groups * batches,)),
+            dma((groups,)), dma((groups,)),
+            dma((batches,)), dma((batches,)),
+            dma(((chunks + 1) * depth,)), dma(((chunks + 1) * depth,)),
+            dma(((chunks + 1) * depth,)), dma(((chunks + 1) * depth,)),
+            dma((2,)),
+        ],
+        compiler_params=pltpu.CompilerParams(
+            collective_id=0, has_side_effects=True, vmem_limit_bytes=40 * 1024 * 1024
+        ),
+        cost_estimate=pl.CostEstimate(flops=20_000_000, bytes_accessed=12_000_000, transcendentals=0),
+    )(messages, probe_blocks, own_objects, own_probe)
 
 
 def local(objects, probe, measured, send_list, corner_slot, offsets):
     length = probe.shape[-1]
     half = probe.shape[0] // 2
     groups = lax.axis_size("tile")
+    batches = lax.axis_size("batch")
     row_block = length // groups
     cut = lax.axis_index("cuts")
     fresnel, farfield = transform_tables(length)
@@ -95,23 +287,41 @@
     probe_term = jnp.roll(probe_term, (-y0, -x0), axis=(2, 3))
     grad = jnp.where(first, g0, g1) + swap(jnp.where(first, g1, g0), "cuts")
 
-    slot_grads = jnp.stack([jnp.where(slot_plane == o, grad, 0.0) for o in range(groups)])
-    probe_blocks = probe_term.reshape(half * 2, groups, row_block, length)
-    returned = lax.all_to_all(slot_grads, "tile", split_axis=0, concat_axis=0, tiled=True)
-    pieces = lax.all_to_all(probe_blocks, "tile", split_axis=1, concat_axis=1, tiled=True)
-    probe_rows = jnp.sum(pieces, axis=1).reshape(half, 2, row_block, length)
+    rows = length // batches
+    sub = row_block // batches
     tile_count = owned.shape[0]
-    tile_ids = jnp.arange(tile_count, dtype=jnp.int32)[:, None, None, None]
-    tile_term = jnp.where(pick[0] == tile_ids, returned[0][None], 0.0)
-    for s in range(1, groups):
-        tile_term = tile_term + jnp.where(pick[s] == tile_ids, returned[s][None], 0.0)
-    tile_total, probe_total = lax.psum((tile_term, probe_rows), "batch")
-    new_objects = objects - OBJECT_RATE * tile_total[None]
-    row_start = lax.axis_index("tile") * row_block
-    own_probe = lax.dynamic_slice_in_dim(my_probe, row_start, row_block, 2)
-    position_total = lax.axis_size("batch") * groups
-    new_probe = own_probe - PROBE_RATE / math.sqrt(position_total) * probe_total
-    return (new_objects, new_probe)
+    my_batch, my_tile = lax.axis_index("batch"), lax.axis_index("tile")
+    blocks = grad.reshape(2, batches, rows, length).transpose(1, 0, 2, 3)
+    blocks = blocks.reshape(batches, 2 * rows, length)
+    meta_rows = -(-(3 + groups) // 8) * 8
+    start_rows = (y0 - rows * jnp.arange(batches)).astype(jnp.float32)
+    spread = lambda v: jnp.broadcast_to(v.astype(jnp.float32), (batches, length))
+    meta = [
+        spread(jnp.where(cells < x0, slots[1], slots[0])[None]),
+        spread(jnp.where(cells < x0, slots[3], slots[2])[None]),
+        spread(start_rows[:, None]),
+    ]
+    meta += [spread(pick[(my_tile - e) % groups][None, None]) for e in range(groups)]
+    meta += [jnp.zeros((batches, length), jnp.float32)] * (meta_rows - len(meta))
+    messages = jnp.concatenate([blocks, jnp.stack(meta, axis=1)], axis=1)
+    probe_rows = 2 * half * sub
+    probe_blocks = probe_term.reshape(2 * half, groups, batches, sub, length)
+    probe_blocks = probe_blocks.transpose(1, 2, 0, 3, 4).reshape(
+        groups, batches, probe_rows, length
+    )
+    own_objects = lax.dynamic_slice_in_dim(
+        owned.reshape(tile_count * 2, batches, rows, length), my_batch, 1, 1
+    ).reshape(tile_count * 2, rows, length)
+    own_probe = my_probe.reshape(2 * half, groups, batches, sub, length)
+    own_probe = lax.dynamic_slice_in_dim(own_probe, my_tile, 1, 1)
+    own_probe = lax.dynamic_slice_in_dim(own_probe, my_batch, 1, 2)
+    own_probe = own_probe.reshape(probe_rows, length)
+    objects_out, probe_out = reduce_and_gather(
+        messages, probe_blocks, own_objects, own_probe, batches, groups, rows
+    )
+    new_objects = objects_out.reshape(objects.shape)
+    new_probe = probe_out.reshape(batches, 2 * half, sub, length).transpose(1, 0, 2, 3)
+    return (new_objects, new_probe.reshape(half, 2, row_block, length))
 
 
 def solution(mesh):

time: 289 us -> 184 us (0.64); the launches traced: 284 us -> 183 us
  waiting for transfers between devices: 201 us -> 8.7 us
  Pallas kernels: 0 us -> 94.4 us
  local copies, waits for them, and re-layouts: 11.1 us -> 27.9 us
  between operations: 19.8 us -> 7.52 us
  other arithmetic: 29.1 us -> 20.7 us
  matrix products: 12.2 us -> 19.9 us
  starting transfers between devices: 11.4 us -> 4.09 us
    psum x1 -> x0, waiting for transfers between devices: 168 us -> none  [local(): tile_total, probe_total = lax.psum((tile_term, probe_rows), 'batch')]
    pallas_call x0 -> x1, Pallas kernels: none -> 94.4 us  [reduce_and_gather(): pl.pallas_call(functools.partial(reduce_kernel, batches, groups, rows, ch...]
    all_to_all x2 -> x0, waiting for transfers between devices: 24.1 us -> none  [the longest x1 13.2 us: local(): lax.all_to_all(probe_blocks, 'tile', split_axis=1, concat_axis=1, tiled=T...]
    sub x2 -> x0, other arithmetic: 8.09 us -> none  [the longest x1 6.14 us: local(): new_objects = objects - OBJECT_RATE * tile_total[None]]
    dot_general x8, matrix products: 12.2 us -> 19.9 us  [the longest x4 12.5 us: apply_both(): done = jnp.einsum('jk,mkl->mjl', left, tall, precision=EXACT)]
    all_to_all x2 -> x0, starting transfers between devices: 7.16 us -> none  [the longest x1 3.58 us: local(): lax.all_to_all(slot_grads, 'tile', split_axis=0, concat_axis=0, tiled=True)]
    unnamed x39 -> x64, local copies, waits for them, and re-layouts: 2.54 us -> 9.45 us
    convert_element_type x0 -> x2, other arithmetic: none -> 3.71 us  [the longest x1 3.08 us: local(): v.astype(jnp.float32)]
  transfers between devices with their start and end apart: 7 -> 4, of which waited for: 4 -> 1; matrix products, arithmetic and copies ran while one was open for 5% -> 8% of each run, Pallas kernels for 0% -> 0%
where the time goes in v2:
time: 184 us; the launch traced here: 183 us
  Pallas kernels  94.4 us (51%)
  local copies, waits for them, and re-layouts  27.9 us (15%)
  other arithmetic  20.7 us (11%)
  matrix products  19.9 us (11%)
  waiting for transfers between devices  8.7 us (5%)
  between operations  7.52 us (4%)
  starting transfers between devices  4.09 us (2%)
    pallas_call x1, Pallas kernels, reduce_and_gather(): pl.pallas_call(functools.partial(reduce_kernel, batches, groups, rows, ch...  94.4 us
    dot_general x4, matrix products, apply_both(): done = jnp.einsum('jk,mkl->mjl', left, tall, precision=EXACT)  12.5 us
    unnamed x64, local copies, waits for them, and re-layouts  9.45 us
    all_to_all x1, waiting for transfers between devices, local(): lax.all_to_all(outgoing, 'tile', split_axis=0, concat_axis=0, tiled=True)  8.7 us
    dot_general x4, matrix products, apply_both(): wide = jnp.einsum('mjk,kl->mjl', stacked, right, precision=EXACT)  7.41 us
  transfers between devices with their start and end apart: 4, of which 1 were waited for; matrix products, arithmetic and copies ran while one was open for 8% of the time, Pallas kernels for 0%

profile of v2, /device:TPU:24, one launch (start us, length us, event | category | flops | bytes accessed | tf_op | source)
XLA Modules:
  0.0 183.2 jit_solution(10583017503869665950)
XLA Ops:
  0.6 0.8 compare_and_fusion
  1.5 0.7 fusion.38
  2.1 2.8 %gather_fusion = f32[2,2,256,256]{3,2,1,0:T(8,128)S(1)} fusion(f32[8,2,256,256]{3,2,1,0:T(8,128)} %bitcast.129, s32[1024]{0:T(1024)S(1)} %pad_clamp_fusion), kind=kCustom, calls=%fused_computation | custom fusion | bytes 2097160 | tf_op jit(solution)/shard_map/jit(_take)/gather | solution.py:254
  5.0 1.1 broadcast_select_fusion
  6.1 3.6 %all-to-all-start = ((f32[2,2,256,256]{3,2,1,0:T(8,128)}), f32[2,2,256,256]{3,2,1,0:T(8,128)S(1)}, u32[]{:S(2)}, u32[]{:S(2)}) async-start(f32[2,2,256,256]{3,2,1,0:T(8,128)} %broadcast_select_fusion), calls=%async_computation | async-start | bytes 2097152 | tf_op jit(solution)/shard_map/all_to_all | solution.py:255
  9.7 0.6 fusion.56
  10.3 0.6 iota_compare_fusion.1
  11.0 0.6 fusion.55
  11.6 3.1 %fusion.47 = (f32[256]{0:T(256)S(1)}, s32[256]{0:T(256)S(1)}, f32[256]{0:T(256)S(1)}, s32[256]{0:T(256)S(1)}) fusion(s32[]{:T(128)} %bitcast.10, s32[]{:T(128)} %bitcast.9, s32[]{:T(128)} %bitcast.4, s32[]{:T(128)} %bitcast.12, s32[]{:T(128)} %bitcast.11), kind=kLoop, calls=%fused_computation.105 | loop fusion | flops 1280 | bytes 4116 | tf_op jit(solution)/shard_map/convert_element_type | solution.py:298
  14.8 8.7 %all-to-all-done = f32[2,2,256,256]{3,2,1,0:T(8,128)S(1)} async-done(((f32[2,2,256,256]{3,2,1,0:T(8,128)}), f32[2,2,256,256]{3,2,1,0:T(8,128)S(1)}, u32[]{:S(2)}, u32[]{:S(2)}) %all-to-all-start) | async-done | bytes 1048608 | tf_op jit(solution)/shard_map/all_to_all | solution.py:255
  23.5 0.9 fusion.34
  28.3 2.0 %fusion.4 = f32[2,2,256,256]{3,2,0,1:T(8,128)} fusion(s32[]{:T(128)S(6)} %select_n.149, s32[]{:T(128)S(6)} %select_n.147, f32[2,2,256,256]{3,2,1,0:T(8,128)S(1)} %constant_dynamic-slice_fusion.3), kind=kLoop, calls=%fused_computation.19 | loop fusion | flops 524288 | bytes 2097160 | tf_op jit(solution)/shard_map/jit(_roll_dynamic)/concatenate | solution.py:275
  30.3 2.0 %broadcast_select_fusion.2 = (f32[2,256,256]{2,1,0:T(8,128)S(1)}, f32[2,256,256]{2,1,0:T(8,128)}) fusion(f32[2,256,256]{2,1,0:T(8,128)} %collective-permute-done, pred[]{:T(512)S(6)} %eq.15, f32[2,2,256,256]{3,2,1,0:T(8,128)S(1)} %all-to-all-done, pred[256,256]{1,0:T(8,128)(4,1)S(1)} %select_compare_fusion), kind=kLoop, calls=%fused_computation.82 | loop fusion | flops 393216 | bytes 2686977 | tf_op jit(solution)/shard_map/jit(_where)/select_n | solution.py:271
  32.3 0.8 slice_bitcast_fusion.7
  33.1 1.1 copy.68
  34.2 1.8 copy.70
  36.0 1.2 slice_bitcast_fusion.6
  38.0 1.8 %fusion.6 = f32[2,256,512]{2,1,0:T(8,128)S(1)} fusion(f32[512,512,1]{1,0,2:T(8,128)S(1)} %copy-done.8, f32[2,256,256]{2,1,0:T(8,128)S(1)} %get-tuple-element.22, f32[2,256,256]{2,1,0:T(8,128)S(1)} %get-tuple-element.21), kind=kOutput, calls=%fused_computation.21 | convolution fusion | flops 1610874880 | bytes 3145728 | tf_op jit(solution)/shard_map/mjk,kl->mjl/dot_general | solution.py:46
  40.0 3.5 %convolution_bitcast_fusion.3 = f32[2,512,256]{1,2,0:T(8,128)S(1)} fusion(f32[512,512,1]{1,0,2:T(8,128)S(1)} %copy-done.10, f32[2,256,256]{2,1,0:T(8,128)S(1)} %get-tuple-element.38, f32[2,256,256]{2,1,0:T(8,128)S(1)} %get-tuple-element.37), kind=kOutput, calls=%fused_computation.14 | convolution fusion | flops 1610874880 | bytes 3145728 | tf_op jit(solution)/shard_map/jk,mkl->mjl/dot_general | solution.py:48
  43.6 1.5 copy-done.12
  45.1 1.8 %fusion.13 = f32[2,256,512]{2,1,0:T(8,128)S(1)} fusion(f32[512,512,1]{1,0,2:T(8,128)S(1)} %copy-done.12, f32[2,256,256]{1,2,0:T(8,128)S(1)} %get-tuple-element.20, f32[2,256,256]{1,2,0:T(8,128)S(1)} %get-tuple-element.19), kind=kOutput, calls=%fused_computation.28 | convolution fusion | flops 1610874880 | bytes 3145728 | tf_op jit(solution)/shard_map/mjk,kl->mjl/dot_general | solution.py:46
  47.0 3.7 %convolution_bitcast_fusion.2 = f32[2,512,256]{1,2,0:T(8,128)S(1)} fusion(f32[512,512,1]{1,0,2:T(8,128)S(1)} %copy-done.14, f32[2,256,256]{2,1,0:T(8,128)S(1)} %get-tuple-element.34, f32[2,256,256]{2,1,0:T(8,128)S(1)} %get-tuple-element.33), kind=kOutput, calls=%fused_computation.13 | convolution fusion | flops 1610874880 | bytes 3145728 | tf_op jit(solution)/shard_map/jk,mkl->mjl/dot_general | solution.py:48
  50.7 0.8 add_reduce_fusion.2
  52.0 1.8 copy.73
  53.8 1.2 bitcast_subtract_fusion
  55.2 1.8 %fusion.20 = f32[2,256,512]{2,1,0:T(8,128)S(1)} fusion(f32[512,512,1]{1,0,2:T(8,128)S(1)} %copy-done.15, f32[2,256,256]{1,2,0:T(8,128)S(1)} %get-tuple-element.24, f32[2,256,256]{1,2,0:T(8,128)S(1)} %get-tuple-element.23), kind=kOutput, calls=%fused_computation.35 | convolution fusion | flops 1610874880 | bytes 3145728 | tf_op jit(solution)/shard_map/mjk,kl->mjl/dot_general | solution.py:46
  57.2 3.5 %convolution_bitcast_fusion.1 = f32[2,512,256]{1,2,0:T(8,128)S(1)} fusion(f32[512,512,1]{1,0,2:T(8,128)S(1)} %copy-done.13, f32[2,256,256]{2,1,0:T(8,128)S(1)} %get-tuple-element.32, f32[2,256,256]{2,1,0:T(8,128)S(1)} %get-tuple-element.31), kind=kOutput, calls=%fused_computation.12 | convolution fusion | flops 1610874880 | bytes 3145728 | tf_op jit(solution)/shard_map/jk,mkl->mjl/dot_general | solution.py:48
  60.7 1.0 multiply_add_fusion
  62.0 1.9 %fusion.27 = f32[2,256,512]{2,1,0:T(8,128)S(1)} fusion(f32[512,512,1]{1,0,2:T(8,128)S(1)} %copy-done.11, f32[2,256,256]{1,2,0:T(8,128)S(1)} %get-tuple-element.18, f32[2,256,256]{1,2,0:T(8,128)S(1)} %get-tuple-element.17), kind=kOutput, calls=%fused_computation.42 | convolution fusion | flops 1610874880 | bytes 3145728 | tf_op jit(solution)/shard_map/mjk,kl->mjl/dot_general | solution.py:46
  64.0 1.9 %convolution_bitcast_fusion = f32[2,512,256]{2,1,0:T(8,128)S(1)} fusion(f32[512,512,1]{1,0,2:T(8,128)S(1)} %copy-done.9, f32[2,256,256]{2,1,0:T(8,128)S(1)} %get-tuple-element.28, f32[2,256,256]{2,1,0:T(8,128)S(1)} %get-tuple-element.27), kind=kOutput, calls=%fused_computation.11 | convolution fusion | flops 1610874880 | bytes 3145728 | tf_op jit(solution)/shard_map/jk,mkl->mjl/dot_general | solution.py:48
  65.9 1.3 subtract_bitcast_fusion
  67.2 1.2 copy.80
  68.5 0.9 fusion.35
  69.4 0.6 subtract_convert_fusion
  71.4 0.6 constant_dynamic-slice_fusion.1
  73.1 0.9 constant_dynamic-slice_fusion
  74.0 1.9 %dynamic-slice_bitcast_fusion.own_obj = f32[16,32,256]{2,1,0:T(8,128)} fusion(f32[16,8,32,256]{3,2,1,0:T(8,128)} %bitcast.130, s32[]{:T(128)S(6)} %select_n.138), kind=kLoop, calls=%fused_computation.56 | loop fusion | bytes 1048580 | tf_op jit(solution)/shard_map/reshape | solution.py:314
  75.9 1.6 fusion.2
  77.5 0.6 fusion
  78.3 0.7 copy-done.19
  79.2 1.1 select_add_fusion
  80.4 0.8 copy.81
  81.4 2.5 %concatenate.52.msg = f32[8,72,256]{2,1,0:T(8,128)} concatenate(f32[8,64,256]{2,1,0:T(8,128)} %bitcast.128, f32[8,1,256]{2,1,0:T(1,128)S(1)} %stack_broadcast_in_dim.32, f32[8,1,256]{2,1,0:T(1,128)S(1)} %stack_broadcast_in_dim.33, f32[8,1,256]{2,1,0:T(1,128)S(1)} %stack_broadcast_in_dim.34, f32[8,1,256]{2,1,0:T(1,128)S(1)} %stack_broadcast_in_dim.36, ...), dimensions={1} | concatenate | bytes 1179648 | tf_op jit(solution)/shard_map/concatenate | solution.py:306
  83.8 1.1 copy-done.1
  84.9 1.0 copy-done.2
  86.0 94.4 %shard_map.149 = (f32[16,8,32,256]{3,2,1,0:T(8,128)S(1)}, f32[8,64,256]{2,1,0:T(8,128)S(1)}) custom-call(f32[8,72,256]{2,1,0:T(8,128)S(1)} %copy-done.1, f32[2,8,64,256]{3,2,1,0:T(8,128)S(1)} %bitcast.114, f32[16,32,256]{2,1,0:T(8,128)S(1)} %copy-done.2, f32[64,256]{1,0:T(8,128)S(1)} %bitcast.116), custom_call_target="tpu_custom_call" | custom-call | flops 20000000 | bytes 12000000 | tf_op jit(solution)/shard_map/pallas_call | solution.py:214
  180.3 0.8 copy.86
  181.2 2.0 %copy.102 = f32[1,8,2,256,256]{4,3,2,1,0:T(8,128)} copy(f32[1,8,2,256,256]{4,3,2,1,0:T(8,128)S(1)} %bitcast.113) | data formatting | bytes 8388608
  (84 shorter events, 3.2 us)
Async XLA Ops:
  0.6 27.6 %copy-start = (f32[4,2,256,256]{3,2,1,0:T(8,128)S(1)}, f32[4,2,256,256]{3,2,1,0:T(8,128)}, u32[]{:S(2)}) copy-start(f32[4,2,256,256]{3,2,1,0:T(8,128)} %param.17) | copy-start | bytes 6291460
  4.9 4.8 %copy-start.30 = (s32[1,2]{1,0:T(1,128)S(1)}, s32[1,2]{1,0:T(1,128)}, u32[]{:S(2)}) copy-start(s32[1,2]{1,0:T(1,128)} %param.21) | copy-start | bytes 28
  4.9 6.0 %copy-start.28 = (s32[1,4]{1,0:T(1,128)S(1)}, s32[1,4]{1,0:T(1,128)}, u32[]{:S(2)}) copy-start(s32[1,4]{1,0:T(1,128)} %param.20) | copy-start | bytes 52
  6.1 17.4 %all-to-all-start = ((f32[2,2,256,256]{3,2,1,0:T(8,128)}), f32[2,2,256,256]{3,2,1,0:T(8,128)S(1)}, u32[]{:S(2)}, u32[]{:S(2)}) async-start(f32[2,2,256,256]{3,2,1,0:T(8,128)} %broadcast_select_fusion), calls=%async_computation | async-start | bytes 2097152 | tf_op jit(solution)/shard_map/all_to_all | solution.py:255
  24.4 5.9 %collective-permute-start = (f32[2,256,256]{2,1,0:T(8,128)}, f32[2,256,256]{2,1,0:T(8,128)}, u32[]{:S(2)}, u32[]{:S(2)}) collective-permute-start(f32[2,256,256]{2,1,0:T(8,128)} %fusion.34), channel_id=1, source_target_pairs={{0,1},{1,0},{2,3},{3,2},{4,5},{5,4},{6,7},{7,6},{8,9},{9,8},{10,11... | collective-permute-start | bytes 1572872 | tf_op jit(solution)/shard_map/ppermute | solution.py:53
  28.3 4.0 %copy-start.7 = (f32[2,2,256,256]{3,2,1,0:T(8,128)}, f32[2,2,256,256]{3,2,1,0:T(8,128)S(1)}, u32[]{:S(2)}) copy-start(f32[2,2,256,256]{3,2,1,0:T(8,128)S(1)} %constant_dynamic-slice_fusion.3) | copy-start | bytes 3145732
  32.3 4.9 %copy-start.5 = (f32[2,2,256,256]{3,2,0,1:T(8,128)S(1)}, f32[2,2,256,256]{3,2,0,1:T(8,128)}, u32[]{:S(2)}) copy-start(f32[2,2,256,256]{3,2,0,1:T(8,128)} %fusion.4) | copy-start | bytes 3145732
  36.0 2.0 %copy-start.8 = (f32[512,512,1]{1,0,2:T(8,128)S(1)}, f32[512,512,1]{1,0,2:T(8,128)}, u32[]{:S(2)}) copy-start(f32[512,512,1]{1,0,2:T(8,128)} %constant.122) | copy-start | bytes 3145732
  37.1 0.7 copy-start.20
  37.2 0.8 copy-start.22
  38.0 2.0 %copy-start.10 = (f32[512,512,1]{1,0,2:T(8,128)S(1)}, f32[512,512,1]{1,0,2:T(8,128)}, u32[]{:S(2)}) copy-start(f32[512,512,1]{1,0,2:T(8,128)} %constant.123) | copy-start | bytes 3145732
  39.9 3.5 %copy-start.16 = (f32[256,256]{0,1:T(8,128)S(1)}, f32[256,256]{0,1:T(8,128)}, u32[]{:S(2)}) copy-start(f32[256,256]{0,1:T(8,128)} %copy.70) | copy-start | bytes 786436
  43.4 3.5 %copy-start.3 = (f32[2,512,256]{1,2,0:T(8,128)}, f32[2,512,256]{1,2,0:T(8,128)S(1)}, u32[]{:S(2)}) copy-start(f32[2,512,256]{1,2,0:T(8,128)S(1)} %convolution_bitcast_fusion.3) | copy-start | bytes 3145732
  43.5 1.6 copy-start.12
  45.1 2.0 %copy-start.14 = (f32[512,512,1]{1,0,2:T(8,128)S(1)}, f32[512,512,1]{1,0,2:T(8,128)}, u32[]{:S(2)}) copy-start(f32[512,512,1]{1,0,2:T(8,128)} %constant.125) | copy-start | bytes 3145732
  51.5 2.3 %collective-permute-start.1 = (f32[256,256]{0,1:T(8,128)}, f32[256,256]{0,1:T(8,128)}, u32[]{:S(2)}, u32[]{:S(2)}) collective-permute-start(f32[256,256]{0,1:T(8,128)} %add_reduce_fusion.2), channel_id=1, source_target_pairs={{0,1},{1,0},{2,3},{3,2},{4,5},{5,4},{6,7},{7,6},{8,9},{9,8},{10,11... | collective-permute-start | bytes 786440 | tf_op jit(solution)/shard_map/ppermute | solution.py:53
  53.8 1.5 copy-start.15
  55.2 2.0 %copy-start.13 = (f32[512,512,1]{1,0,2:T(8,128)S(1)}, f32[512,512,1]{1,0,2:T(8,128)}, u32[]{:S(2)}) copy-start(f32[512,512,1]{1,0,2:T(8,128)} %constant.124) | copy-start | bytes 3145732
  57.2 3.5 %copy-start.4 = (f32[2,512,256]{1,2,0:T(8,128)S(1)}, f32[2,512,256]{1,2,0:T(8,128)}, u32[]{:S(2)}) copy-start(f32[2,512,256]{1,2,0:T(8,128)} %copy-done.3) | copy-start | bytes 3145732
  57.2 3.5 %copy-start.17 = (f32[256,256]{0,1:T(8,128)S(1)}, f32[256,256]{0,1:T(8,128)}, u32[]{:S(2)}) copy-start(f32[256,256]{0,1:T(8,128)} %copy.70) | copy-start | bytes 786436
  60.7 1.3 copy-start.11
  62.0 2.0 %copy-start.9 = (f32[512,512,1]{1,0,2:T(8,128)S(1)}, f32[512,512,1]{1,0,2:T(8,128)}, u32[]{:S(2)}) copy-start(f32[512,512,1]{1,0,2:T(8,128)} %constant.122) | copy-start | bytes 3145732
  64.0 1.9 %copy-start.6 = (f32[2,2,256,256]{3,2,0,1:T(8,128)S(1)}, f32[2,2,256,256]{3,2,0,1:T(8,128)}, u32[]{:S(2)}) copy-start(f32[2,2,256,256]{3,2,0,1:T(8,128)} %fusion.4) | copy-start | bytes 3145732
  64.0 1.9 %copy-start.21 = (f32[256,256]{1,0:T(8,128)S(1)}, f32[256,256]{1,0:T(8,128)}, u32[]{:S(2)}) copy-start(f32[256,256]{1,0:T(8,128)} %copy-done.20) | copy-start | bytes 786436
  64.0 1.9 %copy-start.23 = (f32[256,256]{1,0:T(8,128)S(1)}, f32[256,256]{1,0:T(8,128)}, u32[]{:S(2)}) copy-start(f32[256,256]{1,0:T(8,128)} %copy-done.22) | copy-start | bytes 786436
  67.2 5.9 %copy-start.18 = (f32[256,256]{1,0:T(8,128)}, f32[256,256]{1,0:T(8,128)S(1)}, u32[]{:S(2)}) copy-start(f32[256,256]{1,0:T(8,128)S(1)} %get-tuple-element.26) | copy-start | bytes 786436
  67.2 4.2 %copy-start.29 = (s32[1,1,2]{2,1,0:T(1,128)S(1)}, s32[1,1,2]{2,1,0:T(1,128)}, u32[]{:S(2)}) copy-start(s32[1,1,2]{2,1,0:T(1,128)} %param.19) | copy-start | bytes 28
  68.4 9.1 %copy-start.24 = (f32[256,256]{1,0:T(8,128)}, f32[256,256]{1,0:T(8,128)S(1)}, u32[]{:S(2)}) copy-start(f32[256,256]{1,0:T(8,128)S(1)} %copy.80) | copy-start | bytes 786436
  68.5 9.0 %copy-start.26 = (f32[256,256]{1,0:T(8,128)}, f32[256,256]{1,0:T(8,128)S(1)}, u32[]{:S(2)}) copy-start(f32[256,256]{1,0:T(8,128)S(1)} %copy.79) | copy-start | bytes 786436
  69.4 8.9 %collective-permute-start.2 = (f32[2,256,256]{2,1,0:T(8,128)}, f32[2,256,256]{2,1,0:T(8,128)}, u32[]{:S(2)}, u32[]{:S(2)}) collective-permute-start(f32[2,256,256]{2,1,0:T(8,128)} %fusion.35), channel_id=1, source_target_pairs={{0,1},{1,0},{2,3},{3,2},{4,5},{5,4},{6,7},{7,6},{8,9},{9,8},{10,11... | collective-permute-start | bytes 1572872 | tf_op jit(solution)/shard_map/ppermute | solution.py:53
  78.1 1.0 copy-start.19
  78.1 1.0 copy-start.25
  78.1 1.1 copy-start.27
  83.8 1.1 copy-start.1
  84.9 1.0 copy-start.2

commit v3 on v2

--- a/solution.py
+++ b/solution.py
@@ -25,48 +25,34 @@
     return as_pair(fresnel), as_pair(unitary)
 
 
-def conjugate(matrix):
-    return (matrix[0], -matrix[1])
-
-
-def complex_times(a, b):
-    return (a[0] * b[0] - a[1] * b[1], a[0] * b[1] + a[1] * b[0])
-
-
-def conj_times(a, b):
-    return (a[0] * b[0] + a[1] * b[1], a[0] * b[1] - a[1] * b[0])
-
-
-def apply_both(matrix, field):
+def wide_table(matrix):
     re, im = matrix
-    left = np.concatenate([np.concatenate([re, -im], 1), np.concatenate([im, re], 1)], 0)
-    right = np.concatenate([np.concatenate([re, im], 1), np.concatenate([-im, re], 1)], 0)
-    length = re.shape[0]
-    stacked = jnp.concatenate([field[0], field[1]], axis=-1)
-    wide = jnp.einsum("mjk,kl->mjl", stacked, right, precision=EXACT)
-    tall = jnp.concatenate([wide[..., :length], wide[..., length:]], axis=-2)
-    done = jnp.einsum("jk,mkl->mjl", left, tall, precision=EXACT)
-    return (done[:, :length], done[:, length:])
-
-
-def swap(value, axis):
-    return lax.ppermute(value, axis, [(0, 1), (1, 0)])
+    return np.concatenate([np.concatenate([re, im], 1), np.concatenate([-im, re], 1)], 0)
+
+
+def exact_dot(a, b):
+    return jnp.dot(a, b, precision=EXACT, preferred_element_type=jnp.float32)
 
 
 MESH = pl.DeviceIdType.MESH
 
 
-def reduce_kernel(
+def step_kernel(
     batches, groups, rows, chunks,
-    msg, prb, own_obj, own_prb, out_obj, out_prb,
+    outg, vec, probe, meas, meta, fres_l, fres_r, far_l, far_r, own_obj, own_prb,
+    out_obj, out_prb,
+    tin, tt, pp, rot, xin, mid, phi, psi, chi, part, part_in, gg, g_in, pt, msg, prb,
     got, px, ps, py, obj, prn,
+    t_send, t_recv, c_send, c_recv,
     g_send, g_recv, f_send, f_recv, x_send, x_recv, y_send, y_recv,
     a_send, a_recv, b_send, b_recv, l_sem,
 ):
-    me, mine = lax.axis_index("batch"), lax.axis_index("tile")
+    me, mine, cut = lax.axis_index("batch"), lax.axis_index("tile"), lax.axis_index("cuts")
     depth = batches // 2
     pair = me + 1 - 2 * (me % 2)
     tiles = own_obj.shape[0] // 2
+    n = meas.shape[0]
+    half = pp.shape[0]
     behind = lambda d: (me + batches - d) % batches
 
     barrier = pltpu.get_barrier_semaphore()
@@ -78,7 +64,8 @@
         pl.semaphore_signal(
             barrier, inc=1, device_id={"tile": (mine + e) % groups}, device_id_type=MESH
         )
-    pl.semaphore_wait(barrier, batches + groups - 2)
+    pl.semaphore_signal(barrier, inc=1, device_id={"cuts": 1 - cut}, device_id_type=MESH)
+    pl.semaphore_wait(barrier, batches + groups - 1)
 
     def send(src, dst, sems, place, target):
         copy = pltpu.make_async_remote_copy(
@@ -90,7 +77,155 @@
 
     to_batch = lambda d: {"batch": (me + d) % batches}
     to_tile = lambda e: {"tile": (mine + e) % groups}
-    sent = []
+    other = {"cuts": 1 - cut}
+    tile_copies = [
+        send(outg.at[(mine + e) % groups], tin.at[e], (t_send, t_recv), e, to_tile(e))
+        for e in range(1, groups)
+    ]
+    tin[0] = outg[mine]
+
+    iota0 = lax.broadcasted_iota(jnp.int32, (n, n), 0).astype(jnp.float32)
+    iota1 = lax.broadcasted_iota(jnp.int32, (n, n), 1).astype(jnp.float32)
+    size = float(n)
+    for k in range(2):
+        shift = vec[pl.ds(2 + k, 1), :]
+        down = iota1 + shift
+        rot[2 * k] = jnp.where(jnp.where(down >= size, down - size, down) == iota0, 1.0, 0.0)
+        side = iota0 + shift
+        rot[2 * k + 1] = jnp.where(jnp.where(side >= size, side - size, side) == iota1, 1.0, 0.0)
+    for m in range(half):
+        for c in range(2):
+            turned = exact_dot(probe[cut * half + m, c], rot[3])
+            pp[m, c] = exact_dot(rot[0], turned)
+
+    def over_rows(step, count=32):
+        def body(i, carry):
+            step(pl.multiple_of(i * count, count), count)
+            return carry
+
+        lax.fori_loop(0, n // count, body, 0)
+
+    for copy in tile_copies:
+        copy.wait()
+
+    def choose(r, h):
+        row = (lax.broadcasted_iota(jnp.int32, (h, n), 0) + r).astype(jnp.float32)
+        slot = jnp.where(row < vec[pl.ds(2, 1), :], vec[pl.ds(1, 1), :], vec[pl.ds(0, 1), :])
+        for c in range(2):
+            value = jnp.zeros((h, n), jnp.float32)
+            for e in range(groups):
+                owner = ((mine + groups - e) % groups).astype(jnp.float32)
+                value = jnp.where(slot == owner, tin[e, c, pl.ds(r, h), :], value)
+            tt[cut, c, pl.ds(r, h), :] = value
+
+    over_rows(choose)
+    tile_swap = send(tt.at[cut], tt.at[cut], (c_send, c_recv), 0, other)
+    tile_swap.wait()
+
+    def put(m, r, h, re, im):
+        xin[pl.ds(m * n + r, h), pl.ds(0, n)] = re
+        xin[pl.ds(m * n + r, h), pl.ds(n, n)] = im
+
+    def take(ref, m, r, h):
+        spot = pl.ds(m * n, n)
+        return ref[pl.ds(r, h), spot], ref[pl.ds(n + r, h), spot]
+
+    def cells(ref, lead, r, h):
+        return ref[lead, 0, pl.ds(r, h), :], ref[lead, 1, pl.ds(r, h), :]
+
+    def times(a, b):
+        return a[0] * b[0] - a[1] * b[1], a[0] * b[1] + a[1] * b[0]
+
+    def conj_times(a, b):
+        return a[0] * b[0] + a[1] * b[1], a[0] * b[1] - a[1] * b[0]
+
+    def transform(left, right, out):
+        for m in range(half):
+            for c in range(2):
+                mid[pl.ds(c * n, n), pl.ds(m * n, n)] = exact_dot(
+                    xin[pl.ds(m * n, n), :], right[:, pl.ds(c * n, n)]
+                )
+        for m in range(half):
+            for c in range(2):
+                out[pl.ds(c * n, n), pl.ds(m * n, n)] = exact_dot(
+                    left[pl.ds(c * n, n), :], mid[:, pl.ds(m * n, n)]
+                )
+
+    def enter(r, h):
+        for m in range(half):
+            put(m, r, h, *times(cells(pp, m, r, h), cells(tt, 0, r, h)))
+
+    over_rows(enter)
+    transform(fres_l, fres_r, phi)
+
+    def second(r, h):
+        for m in range(half):
+            put(m, r, h, *times(cells(tt, 1, r, h), take(phi, m, r, h)))
+
+    over_rows(second)
+    transform(far_l, far_r, psi)
+
+    def brightness(r, h):
+        total = jnp.zeros((h, n), jnp.float32)
+        for m in range(half):
+            re, im = take(psi, m, r, h)
+            total = total + (re * re + im * im)
+        part[pl.ds(r, h), :] = total
+
+    over_rows(brightness)
+    part_swap = send(part, part_in, (c_send, c_recv), 1, other)
+    part_swap.wait()
+
+    def weigh(r, h):
+        rest = part[pl.ds(r, h), :] + part_in[pl.ds(r, h), :] - meas[pl.ds(r, h), :]
+        for m in range(half):
+            re, im = take(psi, m, r, h)
+            put(m, r, h, rest * re, rest * im)
+
+    over_rows(weigh)
+    transform(far_r, far_l, chi)
+
+    def back(r, h):
+        total = (jnp.zeros((h, n), jnp.float32),) * 2
+        for m in range(half):
+            wave = take(chi, m, r, h)
+            term = conj_times(take(phi, m, r, h), wave)
+            total = (total[0] + term[0], total[1] + term[1])
+            put(m, r, h, *conj_times(cells(tt, 1, r, h), wave))
+        for c in range(2):
+            gg[1, c, pl.ds(r, h), :] = total[c]
+
+    over_rows(back)
+    transform(fres_r, fres_l, psi)
+
+    def close(r, h):
+        total = (jnp.zeros((h, n), jnp.float32),) * 2
+        for m in range(half):
+            wave = take(psi, m, r, h)
+            term = conj_times(cells(pp, m, r, h), wave)
+            total = (total[0] + term[0], total[1] + term[1])
+            term = conj_times(cells(tt, 0, r, h), wave)
+            for c in range(2):
+                pt[2 * m + c, pl.ds(r, h), :] = term[c]
+        for c in range(2):
+            gg[0, c, pl.ds(r, h), :] = total[c]
+
+    over_rows(close)
+    grad_swap = send(gg.at[1 - cut], g_in, (c_send, c_recv), 2, other)
+    sub = prb.shape[2] // (2 * half)
+    for k in range(2 * half):
+        turned = exact_dot(rot[1], exact_dot(pt[k], rot[2]))
+        for t in range(groups):
+            for b in range(batches):
+                start = (t * batches + b) * sub
+                prb[t, b, pl.ds(k * sub, sub), :] = turned[start : start + sub]
+    grad_swap.wait()
+    for b in range(batches):
+        for c in range(2):
+            spot = pl.ds(b * rows, rows)
+            msg[b, pl.ds(c * rows, rows), :] = gg[cut, c, spot, :] + g_in[c, spot, :]
+        msg[b, pl.ds(2 * rows, meta.shape[1]), :] = meta[b]
+
     first = {}
     halves = []
     for e in range(1, groups):
@@ -203,29 +338,55 @@
         copy.wait()
 
 
-def reduce_and_gather(messages, probe_blocks, own_objects, own_probe, batches, groups, rows):
-    length = messages.shape[-1]
+def run_step(outgoing, vectors, probe, measured, meta, own_objects, own_probe, sizes):
+    batches, groups, rows, half = sizes
+    length = probe.shape[-1]
+    fresnel, farfield = transform_tables(length)
+    fres_r, far_r = wide_table(fresnel), wide_table(farfield)
+    tables = [fres_r.T.copy(), fres_r, far_r.T.copy(), far_r]
     chunks = 4
     depth = batches // 2
     dma = pltpu.SemaphoreType.DMA
     f32 = jnp.float32
     probe_rows = own_probe.shape[0]
+    message = (2 * rows + meta.shape[1], length)
     vmem = pl.BlockSpec(memory_space=pltpu.VMEM)
+    anywhere = pl.BlockSpec(memory_space=pl.ANY)
+    square = (length, length)
+    field = (2 * length, half * length)
     return pl.pallas_call(
-        functools.partial(reduce_kernel, batches, groups, rows, chunks),
+        functools.partial(step_kernel, batches, groups, rows, chunks),
         out_shape=(
             jax.ShapeDtypeStruct((own_objects.shape[0], batches, rows, length), f32),
             jax.ShapeDtypeStruct((batches, probe_rows, length), f32),
         ),
-        in_specs=[vmem] * 4,
-        out_specs=(pl.BlockSpec(memory_space=pl.ANY), pl.BlockSpec(memory_space=pl.ANY)),
+        in_specs=[vmem] * 11,
+        out_specs=(anywhere, anywhere),
         scratch_shapes=[
-            pltpu.VMEM((groups, batches) + messages.shape[1:], f32),
+            pltpu.VMEM((groups, 2) + square, f32),
+            pltpu.VMEM((2, 2) + square, f32),
+            pltpu.VMEM((half, 2) + square, f32),
+            pltpu.VMEM((4,) + square, f32),
+            pltpu.VMEM((half * length, 2 * length), f32),
+            pltpu.VMEM(field, f32),
+            pltpu.VMEM(field, f32),
+            pltpu.VMEM(field, f32),
+            pltpu.VMEM(field, f32),
+            pltpu.VMEM(square, f32),
+            pltpu.VMEM(square, f32),
+            pltpu.VMEM((2, 2) + square, f32),
+            pltpu.VMEM((2,) + square, f32),
+            pltpu.VMEM((2 * half,) + square, f32),
+            pltpu.VMEM((batches,) + message, f32),
+            pltpu.VMEM((groups, batches, probe_rows, length), f32),
+            pltpu.VMEM((groups, batches) + message, f32),
             pltpu.VMEM((groups, batches, probe_rows, length), f32),
             pltpu.VMEM((batches, probe_rows, length), f32),
             pltpu.VMEM((batches, probe_rows, length), f32),
             pltpu.VMEM(own_objects.shape, f32),
             pltpu.VMEM(own_probe.shape, f32),
+            dma((groups,)), dma((groups,)),
+            dma((3,)), dma((3,)),
             dma((batches,)), dma((batches,)),
             dma((groups * batches,)), dma((groups * batches,)),
             dma((groups,)), dma((groups,)),
@@ -235,10 +396,12 @@
             dma((2,)),
         ],
         compiler_params=pltpu.CompilerParams(
-            collective_id=0, has_side_effects=True, vmem_limit_bytes=40 * 1024 * 1024
+            collective_id=0, has_side_effects=True, vmem_limit_bytes=56 * 1024 * 1024
         ),
-        cost_estimate=pl.CostEstimate(flops=20_000_000, bytes_accessed=12_000_000, transcendentals=0),
-    )(messages, probe_blocks, own_objects, own_probe)
+        cost_estimate=pl.CostEstimate(
+            flops=14_000_000_000, bytes_accessed=20_000_000, transcendentals=0
+        ),
+    )(outgoing, vectors, probe, measured, meta, *tables, own_objects, own_probe)
 
 
 def local(objects, probe, measured, send_list, corner_slot, offsets):
@@ -248,67 +411,29 @@
     batches = lax.axis_size("batch")
     row_block = length // groups
     cut = lax.axis_index("cuts")
-    fresnel, farfield = transform_tables(length)
     owned = objects[0]
     pick = send_list[0, 0]
-    outgoing = jnp.take(owned, pick, axis=0)
-    arrived = lax.all_to_all(outgoing, "tile", split_axis=0, concat_axis=0, tiled=True)
-
+    outgoing = jnp.take(owned, pick, axis=0, mode="clip")
     y0, x0 = offsets[0, 0], offsets[0, 1]
     cells = jnp.arange(length, dtype=jnp.int32)
-    low_row = (cells < y0)[:, None]
-    low_col = (cells < x0)[None, :]
     slots = corner_slot[0]
-    slot_plane = jnp.where(
-        low_row, jnp.where(low_col, slots[3], slots[2]), jnp.where(low_col, slots[1], slots[0])
-    )
-    tile_own = arrived[0]
-    for o in range(1, groups):
-        tile_own = jnp.where(slot_plane == o, arrived[o], tile_own)
-    tile_other = swap(tile_own, "cuts")
-    first = cut == 0
-    t0 = jnp.where(first, tile_own, tile_other)
-    t1 = jnp.where(first, tile_other, tile_own)
-    t0 = (t0[0][None], t0[1][None])
-    t1 = (t1[0][None], t1[1][None])
     my_probe = lax.dynamic_slice_in_dim(probe, cut * half, half, 0)
-    rolled = jnp.roll(my_probe, (y0, x0), axis=(2, 3))
-    p = (rolled[:, 0], rolled[:, 1])
-
-    phi = apply_both(fresnel, complex_times(p, t0))
-    psi = apply_both(farfield, complex_times(t1, phi))
-    part = jnp.sum(psi[0] * psi[0] + psi[1] * psi[1], axis=0)
-    resid = (part + swap(part, "cuts")) - measured[0]
-    chi = apply_both(conjugate(farfield), (resid[None] * psi[0], resid[None] * psi[1]))
-    g1 = jnp.stack([jnp.sum(v, axis=0) for v in conj_times(phi, chi)])
-    zeta = apply_both(conjugate(fresnel), conj_times(t1, chi))
-    g0 = jnp.stack([jnp.sum(v, axis=0) for v in conj_times(p, zeta)])
-    probe_term = jnp.stack(conj_times(t0, zeta), axis=1)
-    probe_term = jnp.roll(probe_term, (-y0, -x0), axis=(2, 3))
-    grad = jnp.where(first, g0, g1) + swap(jnp.where(first, g1, g0), "cuts")
-
     rows = length // batches
     sub = row_block // batches
     tile_count = owned.shape[0]
     my_batch, my_tile = lax.axis_index("batch"), lax.axis_index("tile")
-    blocks = grad.reshape(2, batches, rows, length).transpose(1, 0, 2, 3)
-    blocks = blocks.reshape(batches, 2 * rows, length)
     meta_rows = -(-(3 + groups) // 8) * 8
-    start_rows = (y0 - rows * jnp.arange(batches)).astype(jnp.float32)
+    upper = jnp.where(cells < x0, slots[1], slots[0])
+    lower = jnp.where(cells < x0, slots[3], slots[2])
+    as_row = lambda v: jnp.broadcast_to(v.astype(jnp.float32), (length,))
+    vectors = jnp.stack([as_row(v) for v in (upper, lower, y0, x0)] + [as_row(0 * y0)] * 4)
+    start_rows = y0 - rows * jnp.arange(batches)
     spread = lambda v: jnp.broadcast_to(v.astype(jnp.float32), (batches, length))
-    meta = [
-        spread(jnp.where(cells < x0, slots[1], slots[0])[None]),
-        spread(jnp.where(cells < x0, slots[3], slots[2])[None]),
-        spread(start_rows[:, None]),
-    ]
+    meta = [spread(upper[None]), spread(lower[None]), spread(start_rows[:, None])]
     meta += [spread(pick[(my_tile - e) % groups][None, None]) for e in range(groups)]
     meta += [jnp.zeros((batches, length), jnp.float32)] * (meta_rows - len(meta))
-    messages = jnp.concatenate([blocks, jnp.stack(meta, axis=1)], axis=1)
+    meta = jnp.stack(meta, axis=1)
     probe_rows = 2 * half * sub
-    probe_blocks = probe_term.reshape(2 * half, groups, batches, sub, length)
-    probe_blocks = probe_blocks.transpose(1, 2, 0, 3, 4).reshape(
-        groups, batches, probe_rows, length
-    )
     own_objects = lax.dynamic_slice_in_dim(
         owned.reshape(tile_count * 2, batches, rows, length), my_batch, 1, 1
     ).reshape(tile_count * 2, rows, length)
@@ -316,8 +441,9 @@
     own_probe = lax.dynamic_slice_in_dim(own_probe, my_tile, 1, 1)
     own_probe = lax.dynamic_slice_in_dim(own_probe, my_batch, 1, 2)
     own_probe = own_probe.reshape(probe_rows, length)
-    objects_out, probe_out = reduce_and_gather(
-        messages, probe_blocks, own_objects, own_probe, batches, groups, rows
+    objects_out, probe_out = run_step(
+        outgoing, vectors, probe, measured[0], meta, own_objects, own_probe,
+        (batches, groups, rows, half),
     )
     new_objects = objects_out.reshape(objects.shape)
     new_probe = probe_out.reshape(batches, 2 * half, sub, length).transpose(1, 0, 2, 3)

time: 184 us -> 163 us (0.89)
  Pallas kernels: 94.4 us -> 133 us
  matrix products: 19.9 us -> 0 us
  other arithmetic: 20.7 us -> 7.78 us
  local copies, waits for them, and re-layouts: 27.9 us -> 18.5 us
  waiting for transfers between devices: 8.7 us -> 0 us
  between operations: 7.52 us -> 3.37 us
  starting transfers between devices: 4.09 us -> 0 us
    pallas_call x1, Pallas kernels: 94.4 us -> 133 us  [run_step(): pl.pallas_call(functools.partial(step_kernel, batches, groups, rows, chun...]
    dot_general x8 -> x0, matrix products: 19.9 us -> none  [the longest x4 12.5 us: apply_both(): done = jnp.einsum('jk,mkl->mjl', left, tall, precision=EXACT)]
    all_to_all x1 -> x0, waiting for transfers between devices: 8.7 us -> none  [local(): lax.all_to_all(outgoing, 'tile', split_axis=0, concat_axis=0, tiled=True)]
    convert_element_type x1 -> x2, other arithmetic: 0.62 us -> 6.47 us  [local(): as_row = lambda v: jnp.broadcast_to(v.astype(jnp.float32), (length,))]
    select_n x5 -> x0, other arithmetic: 5.5 us -> none  [the longest x1 1.96 us: local(): t1 = jnp.where(first, tile_other, tile_own)]
    mul x4 -> x0, local copies, waits for them, and re-layouts: 4.85 us -> none  [the longest x2 2.94 us: complex_times(): return (a[0] * b[0] - a[1] * b[1], a[0] * b[1] + a[1] * b[0])]
    unnamed x64 -> x3, local copies, waits for them, and re-layouts: 9.45 us -> 4.6 us
    concatenate x3 -> x0, other arithmetic: 4.22 us -> none  [the longest x2 2.21 us: local(): probe_term = jnp.roll(probe_term, (-y0, -x0), axis=(2, 3))]
  transfers between devices with their start and end apart: 4 -> 0, of which waited for: 1 -> 0; matrix products, arithmetic and copies ran while one was open for 8% -> 0% of each run, Pallas kernels for 0% -> 0%
where the time goes in v3:
time: 163 us; the launch traced here: 162 us
  Pallas kernels  133 us (82%)
  local copies, waits for them, and re-layouts  18.5 us (11%)
  other arithmetic  7.78 us (5%)
  between operations  3.37 us (2%)
    pallas_call x1, Pallas kernels, run_step(): pl.pallas_call(functools.partial(step_kernel, batches, groups, rows, chun...  133 us
    convert_element_type x2, other arithmetic, local(): as_row = lambda v: jnp.broadcast_to(v.astype(jnp.float32), (length,))  6.47 us
    unnamed x3, local copies, waits for them, and re-layouts  4.6 us
    gather x1, local copies, waits for them, and re-layouts, local(): outgoing = jnp.take(owned, pick, axis=0, mode='clip')  3.77 us

profile of v3, /device:TPU:24, one launch (start us, length us, event | category | flops | bytes accessed | tf_op | source)
XLA Modules:
  0.0 162.2 jit_solution(17835814425504965496)
XLA Ops:
  0.6 0.0 copy-start
  0.7 1.4 constant_dynamic-slice_fusion.2
  3.4 1.3 fusion.2
  6.0 0.7 subtract_convert_fusion
  6.7 1.5 fusion.3
  8.2 3.2 %select_convert_fusion = (f32[256]{0:T(256)S(1)}, f32[256]{0:T(256)S(1)}) fusion(s32[]{:T(128)} %bitcast.6, s32[]{:T(128)} %bitcast.5, s32[]{:T(128)} %bitcast.2, s32[]{:T(128)} %bitcast.4, s32[]{:T(128)} %bitcast.3), kind=kLoop, calls=%fused_computation.11 | loop fusion | flops 1280 | bytes 2068 | tf_op jit(solution)/shard_map/convert_element_type | solution.py:428
  11.4 3.2 %fusion = (f32[1,256]{1,0:T(1,128)S(1)}, f32[1,256]{1,0:T(1,128)S(1)}) fusion(s32[]{:T(128)} %bitcast.4, s32[]{:T(128)} %bitcast.3, s32[]{:T(128)} %bitcast.2, s32[]{:T(128)} %bitcast.6, s32[]{:T(128)} %bitcast.5), kind=kLoop, calls=%fused_computation.9 | loop fusion | flops 1280 | bytes 2068 | tf_op jit(solution)/shard_map/convert_element_type | solution.py:428
  14.6 0.7 pad_clamp_fusion
  15.3 0.6 stack.15.vec
  15.9 0.1 stack_broadcast_in_dim.42
  16.1 0.7 stack.17.meta
  16.8 1.9 %dynamic-slice_bitcast_fusion.own_obj = f32[16,32,256]{2,1,0:T(8,128)} fusion(f32[16,8,32,256]{3,2,1,0:T(8,128)} %bitcast.25, s32[]{:T(128)S(6)} %select_n.68), kind=kLoop, calls=%fused_computation.1 | loop fusion | bytes 1048580 | tf_op jit(solution)/shard_map/reshape | solution.py:439
  18.7 3.8 %gather_fusion = f32[2,2,256,256]{3,2,1,0:T(8,128)} fusion(f32[8,2,256,256]{3,2,1,0:T(8,128)} %bitcast.26, s32[1024]{0:T(1024)S(1)} %pad_clamp_fusion), kind=kCustom, calls=%fused_computation | custom fusion | bytes 2097160 | tf_op jit(solution)/shard_map/jit(_take)/gather | solution.py:416
  22.4 0.0 copy-done
  22.5 0.1 constant_dynamic-slice_fusion.1
  22.5 0.6 constant_dynamic-slice_fusion
  23.2 132.6 %shard_map.113 = (f32[16,8,32,256]{3,2,1,0:T(8,128)}, f32[8,64,256]{2,1,0:T(8,128)}) custom-call(f32[2,2,256,256]{3,2,1,0:T(8,128)} %gather_fusion, f32[8,256]{1,0:T(8,128)} %stack.15.vec, f32[4,2,256,256]{3,2,1,0:T(8,128)} %probe.1, f32[256,256]{1,0:T(8,128)} %bitcast.31, f32[8,8,256]{2,1,0:T(8,128)} %stack.17.meta, f32[512,512]{1,0:T(8,128)} %constant.77.clone.fres_l, ...), custom_call_target="tpu_custom_call" | custom-call | flops 14000000000 | bytes 20000000 | tf_op jit(solution)/shard_map/pallas_call | solution.py:357
  155.8 1.9 %copy.15 = f32[4,8,16,256]{3,2,1,0:T(8,128)} copy(f32[4,8,16,256]{3,2,0,1:T(8,128)} %bitcast.27) | data formatting | bytes 1048576 | tf_op jit(solution)/shard_map/transpose | solution.py:449
  157.6 4.6 %copy.18 = f32[1,8,2,256,256]{4,3,2,1,0:T(8,128)} copy(f32[1,8,2,256,256]{4,3,2,1,0:T(8,128)} %bitcast.23) | data formatting | bytes 8388608
  (9 shorter events, 0.1 us)
Async XLA Ops:
  0.6 21.8 %copy-start = (f32[4,2,256,256]{3,2,1,0:T(8,128)S(1)}, f32[4,2,256,256]{3,2,1,0:T(8,128)}, u32[]{:S(2)}) copy-start(f32[4,2,256,256]{3,2,1,0:T(8,128)} %probe.1) | copy-start | bytes 6291460

commit v4 on v3

--- a/solution.py
+++ b/solution.py
@@ -39,9 +39,9 @@
 
 def step_kernel(
     batches, groups, rows, chunks,
-    outg, vec, probe, meas, meta, fres_l, fres_r, far_l, far_r, own_obj, own_prb,
+    pick, corner, offs, objs, probe, meas, fres_l, fres_r, far_l, far_r, own_prb,
     out_obj, out_prb,
-    tin, tt, pp, rot, xin, mid, phi, psi, chi, part, part_in, gg, g_in, pt, msg, prb,
+    outg, tin, tt, pp, rot, xin, mid, phi, psi, chi, part, part_in, gg, g_in, pt, msg, prb,
     got, px, ps, py, obj, prn,
     t_send, t_recv, c_send, c_recv,
     g_send, g_recv, f_send, f_recv, x_send, x_recv, y_send, y_recv,
@@ -50,10 +50,19 @@
     me, mine, cut = lax.axis_index("batch"), lax.axis_index("tile"), lax.axis_index("cuts")
     depth = batches // 2
     pair = me + 1 - 2 * (me % 2)
-    tiles = own_obj.shape[0] // 2
+    tiles = objs.shape[0]
     n = meas.shape[0]
+    y0, x0 = offs[0], offs[1]
+    slots = [corner[k] for k in range(4)]
     half = pp.shape[0]
     behind = lambda d: (me + batches - d) % batches
+
+    def over_rows(step, count=32):
+        def body(i, carry):
+            step(pl.multiple_of(i * count, count), count)
+            return carry
+
+        lax.fori_loop(0, n // count, body, 0)
 
     barrier = pltpu.get_barrier_semaphore()
     for d in range(1, batches):
@@ -65,6 +74,13 @@
             barrier, inc=1, device_id={"tile": (mine + e) % groups}, device_id_type=MESH
         )
     pl.semaphore_signal(barrier, inc=1, device_id={"cuts": 1 - cut}, device_id_type=MESH)
+
+    def fetch(r, h):
+        for t in range(groups):
+            for c in range(2):
+                outg[t, c, pl.ds(r, h), :] = objs[pick[t], c, pl.ds(r, h), :]
+
+    over_rows(fetch)
     pl.semaphore_wait(barrier, batches + groups - 1)
 
     def send(src, dst, sems, place, target):
@@ -84,37 +100,30 @@
     ]
     tin[0] = outg[mine]
 
-    iota0 = lax.broadcasted_iota(jnp.int32, (n, n), 0).astype(jnp.float32)
-    iota1 = lax.broadcasted_iota(jnp.int32, (n, n), 1).astype(jnp.float32)
-    size = float(n)
-    for k in range(2):
-        shift = vec[pl.ds(2 + k, 1), :]
-        down = iota1 + shift
-        rot[2 * k] = jnp.where(jnp.where(down >= size, down - size, down) == iota0, 1.0, 0.0)
-        side = iota0 + shift
-        rot[2 * k + 1] = jnp.where(jnp.where(side >= size, side - size, side) == iota1, 1.0, 0.0)
+    iota0 = lax.broadcasted_iota(jnp.int32, (n, n), 0)
+    iota1 = lax.broadcasted_iota(jnp.int32, (n, n), 1)
+    for k, shift in enumerate((y0, x0)):
+        down, side = iota1 + shift, iota0 + shift
+        rot[2 * k] = jnp.where(jnp.where(down >= n, down - n, down) == iota0, 1.0, 0.0)
+        rot[2 * k + 1] = jnp.where(jnp.where(side >= n, side - n, side) == iota1, 1.0, 0.0)
     for m in range(half):
         for c in range(2):
             turned = exact_dot(probe[cut * half + m, c], rot[3])
             pp[m, c] = exact_dot(rot[0], turned)
 
-    def over_rows(step, count=32):
-        def body(i, carry):
-            step(pl.multiple_of(i * count, count), count)
-            return carry
-
-        lax.fori_loop(0, n // count, body, 0)
-
     for copy in tile_copies:
         copy.wait()
 
     def choose(r, h):
-        row = (lax.broadcasted_iota(jnp.int32, (h, n), 0) + r).astype(jnp.float32)
-        slot = jnp.where(row < vec[pl.ds(2, 1), :], vec[pl.ds(1, 1), :], vec[pl.ds(0, 1), :])
+        low = lax.broadcasted_iota(jnp.int32, (h, n), 0) + r < y0
+        side = lax.broadcasted_iota(jnp.int32, (h, n), 1) < x0
+        slot = jnp.where(
+            low, jnp.where(side, slots[3], slots[2]), jnp.where(side, slots[1], slots[0])
+        )
         for c in range(2):
             value = jnp.zeros((h, n), jnp.float32)
             for e in range(groups):
-                owner = ((mine + groups - e) % groups).astype(jnp.float32)
+                owner = (mine + groups - e) % groups
                 value = jnp.where(slot == owner, tin[e, c, pl.ds(r, h), :], value)
             tt[cut, c, pl.ds(r, h), :] = value
 
@@ -219,12 +228,21 @@
             for b in range(batches):
                 start = (t * batches + b) * sub
                 prb[t, b, pl.ds(k * sub, sub), :] = turned[start : start + sub]
+    meta_rows = msg.shape[1] - 2 * rows
+    real = lambda v: v.astype(jnp.float32)
+    line = lax.broadcasted_iota(jnp.int32, (meta_rows, n), 0)
+    side = lax.broadcasted_iota(jnp.int32, (meta_rows, n), 1) < x0
+    upper = jnp.where(side, real(slots[1]), real(slots[0]))
+    lower = jnp.where(side, real(slots[3]), real(slots[2]))
+    meta = jnp.where(line == 0, upper, lower)
+    for e in range(groups):
+        meta = jnp.where(line == 3 + e, real(pick[(mine + groups - e) % groups]), meta)
     grad_swap.wait()
     for b in range(batches):
         for c in range(2):
             spot = pl.ds(b * rows, rows)
             msg[b, pl.ds(c * rows, rows), :] = gg[cut, c, spot, :] + g_in[c, spot, :]
-        msg[b, pl.ds(2 * rows, meta.shape[1]), :] = meta[b]
+        msg[b, pl.ds(2 * rows, meta_rows), :] = jnp.where(line == 2, real(y0 - rows * b), meta)
 
     first = {}
     halves = []
@@ -286,9 +304,10 @@
                 for j in range(tiles):
                     sums[j] = sums[j] + jnp.where(place == float(j), value, 0.0)
         spot = pl.multiple_of(strip * 8, 8)
+        here = pl.multiple_of(me * rows + strip * 8, 8)
         for j in range(tiles):
             obj[2 * j + plane, pl.ds(spot, 8), :] = (
-                own_obj[2 * j + plane, pl.ds(spot, 8), :] - OBJECT_RATE * sums[j]
+                objs[j, plane, pl.ds(here, 8), :] - OBJECT_RATE * sums[j]
             )
         return carry
 
@@ -338,7 +357,7 @@
         copy.wait()
 
 
-def run_step(outgoing, vectors, probe, measured, meta, own_objects, own_probe, sizes):
+def run_step(pick, corner, offset, owned, probe, measured, own_probe, sizes):
     batches, groups, rows, half = sizes
     length = probe.shape[-1]
     fresnel, farfield = transform_tables(length)
@@ -349,7 +368,9 @@
     dma = pltpu.SemaphoreType.DMA
     f32 = jnp.float32
     probe_rows = own_probe.shape[0]
-    message = (2 * rows + meta.shape[1], length)
+    message = (2 * rows - (-(3 + groups) // 8) * 8, length)
+    block = (2 * owned.shape[0], rows, length)
+    smem = pl.BlockSpec(memory_space=pltpu.SMEM)
     vmem = pl.BlockSpec(memory_space=pltpu.VMEM)
     anywhere = pl.BlockSpec(memory_space=pl.ANY)
     square = (length, length)
@@ -357,12 +378,13 @@
     return pl.pallas_call(
         functools.partial(step_kernel, batches, groups, rows, chunks),
         out_shape=(
-            jax.ShapeDtypeStruct((own_objects.shape[0], batches, rows, length), f32),
+            jax.ShapeDtypeStruct((block[0], batches, rows, length), f32),
             jax.ShapeDtypeStruct((batches, probe_rows, length), f32),
         ),
-        in_specs=[vmem] * 11,
+        in_specs=[smem] * 3 + [vmem] * 8,
         out_specs=(anywhere, anywhere),
         scratch_shapes=[
+            pltpu.VMEM((groups, 2) + square, f32),
             pltpu.VMEM((groups, 2) + square, f32),
             pltpu.VMEM((2, 2) + square, f32),
             pltpu.VMEM((half, 2) + square, f32),
@@ -383,7 +405,7 @@
             pltpu.VMEM((groups, batches, probe_rows, length), f32),
             pltpu.VMEM((batches, probe_rows, length), f32),
             pltpu.VMEM((batches, probe_rows, length), f32),
-            pltpu.VMEM(own_objects.shape, f32),
+            pltpu.VMEM(block, f32),
             pltpu.VMEM(own_probe.shape, f32),
             dma((groups,)), dma((groups,)),
             dma((3,)), dma((3,)),
@@ -396,12 +418,12 @@
             dma((2,)),
         ],
         compiler_params=pltpu.CompilerParams(
-            collective_id=0, has_side_effects=True, vmem_limit_bytes=56 * 1024 * 1024
+            collective_id=0, has_side_effects=True, vmem_limit_bytes=44 * 1024 * 1024
         ),
         cost_estimate=pl.CostEstimate(
             flops=14_000_000_000, bytes_accessed=20_000_000, transcendentals=0
         ),
-    )(outgoing, vectors, probe, measured, meta, *tables, own_objects, own_probe)
+    )(pick, corner, offset, owned, probe, measured, *tables, own_probe)
 
 
 def local(objects, probe, measured, send_list, corner_slot, offsets):
@@ -413,36 +435,16 @@
     cut = lax.axis_index("cuts")
     owned = objects[0]
     pick = send_list[0, 0]
-    outgoing = jnp.take(owned, pick, axis=0, mode="clip")
-    y0, x0 = offsets[0, 0], offsets[0, 1]
-    cells = jnp.arange(length, dtype=jnp.int32)
-    slots = corner_slot[0]
-    my_probe = lax.dynamic_slice_in_dim(probe, cut * half, half, 0)
     rows = length // batches
     sub = row_block // batches
-    tile_count = owned.shape[0]
-    my_batch, my_tile = lax.axis_index("batch"), lax.axis_index("tile")
-    meta_rows = -(-(3 + groups) // 8) * 8
-    upper = jnp.where(cells < x0, slots[1], slots[0])
-    lower = jnp.where(cells < x0, slots[3], slots[2])
-    as_row = lambda v: jnp.broadcast_to(v.astype(jnp.float32), (length,))
-    vectors = jnp.stack([as_row(v) for v in (upper, lower, y0, x0)] + [as_row(0 * y0)] * 4)
-    start_rows = y0 - rows * jnp.arange(batches)
-    spread = lambda v: jnp.broadcast_to(v.astype(jnp.float32), (batches, length))
-    meta = [spread(upper[None]), spread(lower[None]), spread(start_rows[:, None])]
-    meta += [spread(pick[(my_tile - e) % groups][None, None]) for e in range(groups)]
-    meta += [jnp.zeros((batches, length), jnp.float32)] * (meta_rows - len(meta))
-    meta = jnp.stack(meta, axis=1)
-    probe_rows = 2 * half * sub
-    own_objects = lax.dynamic_slice_in_dim(
-        owned.reshape(tile_count * 2, batches, rows, length), my_batch, 1, 1
-    ).reshape(tile_count * 2, rows, length)
-    own_probe = my_probe.reshape(2 * half, groups, batches, sub, length)
-    own_probe = lax.dynamic_slice_in_dim(own_probe, my_tile, 1, 1)
-    own_probe = lax.dynamic_slice_in_dim(own_probe, my_batch, 1, 2)
-    own_probe = own_probe.reshape(probe_rows, length)
+    zero = jnp.zeros((), jnp.int32)
+    own_probe = lax.dynamic_slice(
+        probe.reshape(4 * half, groups, batches, sub, length),
+        (cut * 2 * half, lax.axis_index("tile"), lax.axis_index("batch"), zero, zero),
+        (2 * half, 1, 1, sub, length),
+    ).reshape(2 * half * sub, length)
     objects_out, probe_out = run_step(
-        outgoing, vectors, probe, measured[0], meta, own_objects, own_probe,
+        pick, corner_slot[0], offsets[0], owned, probe, measured[0], own_probe,
         (batches, groups, rows, half),
     )
     new_objects = objects_out.reshape(objects.shape)

time: 163 us -> 148 us (0.908)
  other arithmetic: 7.78 us -> 0 us
  local copies, waits for them, and re-layouts: 18.5 us -> 15.7 us
  between operations: 3.37 us -> 0.65 us
    unnamed x3 -> x19, local copies, waits for them, and re-layouts: 4.6 us -> 14 us
    convert_element_type x3 -> x0, other arithmetic: 7.12 us -> none  [the longest x2 6.47 us: local(): as_row = lambda v: jnp.broadcast_to(v.astype(jnp.float32), (length,))]
    gather x1 -> x0, local copies, waits for them, and re-layouts: 3.77 us -> none  [local(): outgoing = jnp.take(owned, pick, axis=0, mode='clip')]
    slice x2 -> x0, local copies, waits for them, and re-layouts: 2.8 us -> none  [the longest x1 1.46 us: local(): lower = jnp.where(cells < x0, slots[3], slots[2])]
    reshape x1 -> x0, local copies, waits for them, and re-layouts: 1.88 us -> none  [local(): own_objects = lax.dynamic_slice_in_dim(owned.reshape(tile_count * 2, batc...]
where the time goes in v4:
time: 148 us
  Pallas kernels  132 us (89%)
  local copies, waits for them, and re-layouts  15.7 us (11%)
    pallas_call x1, Pallas kernels, run_step(): pl.pallas_call(functools.partial(step_kernel, batches, groups, rows, chun...  132 us
    unnamed x19, local copies, waits for them, and re-layouts  14 us

profile of v4, /device:TPU:24, one launch (start us, length us, event | category | flops | bytes accessed | tf_op | source)
XLA Modules:
  0.0 147.9 jit_solution(1435858761650663054)
XLA Ops:
  0.6 0.9 constant_dynamic-slice_fusion
  1.5 0.0 copy-start
  1.5 1.6 %copy-done = f32[4,2,256,256]{3,2,1,0:T(8,128)S(1)} copy-done((f32[4,2,256,256]{3,2,1,0:T(8,128)S(1)}, f32[4,2,256,256]{3,2,1,0:T(8,128)}, u32[]{:S(2)}) %copy-start) | copy-done | bytes 2097176
  3.1 0.0 copy-start.1
  3.1 0.9 copy-done.1
  4.0 0.0 copy-start.2
  4.0 0.7 copy-done.2
  4.7 0.0 copy-start.3
  4.7 0.7 copy-done.3
  5.3 0.0 copy-start.4
  5.3 0.7 copy-done.4
  6.0 0.0 copy-start.5
  6.0 1.2 copy-done.5
  7.2 0.0 copy-start.6
  7.2 1.2 copy-done.6
  8.5 0.0 copy-start.7
  8.5 1.2 copy-done.7
  9.7 0.0 copy-start.8
  9.7 1.2 copy-done.8
  10.9 131.6 %shard_map.113 = (f32[16,8,32,256]{3,2,1,0:T(8,128)}, f32[8,64,256]{2,1,0:T(8,128)S(1)}) custom-call(s32[2]{0:T(128)S(1)} %bitcast.18, s32[4]{0:T(128)S(1)} %bitcast.19, s32[2]{0:T(128)S(1)} %bitcast.20, f32[8,2,256,256]{3,2,1,0:T(8,128)} %bitcast.23, f32[4,2,256,256]{3,2,1,0:T(8,128)S(1)} %copy-done, f32[256,256]{1,0:T(8,128)S(1)} %bitcast.17, ...), custom_call_target="tpu_custom_call" | custom-call | flops 14000000000 | bytes 20000000 | tf_op jit(solution)/shard_map/pallas_call | solution.py:378
  142.5 0.8 copy.13
  143.3 4.6 %copy.16 = f32[1,8,2,256,256]{4,3,2,1,0:T(8,128)} copy(f32[1,8,2,256,256]{4,3,2,1,0:T(8,128)} %bitcast.21) | data formatting | bytes 8388608
Async XLA Ops:
  1.5 1.6 %copy-start = (f32[4,2,256,256]{3,2,1,0:T(8,128)S(1)}, f32[4,2,256,256]{3,2,1,0:T(8,128)}, u32[]{:S(2)}) copy-start(f32[4,2,256,256]{3,2,1,0:T(8,128)} %probe.1) | copy-start | bytes 6291460
  3.1 0.9 copy-start.1
  4.0 0.7 copy-start.2
  4.7 0.7 copy-start.3
  5.3 0.7 copy-start.4
  6.0 1.2 copy-start.5
  7.2 1.2 copy-start.6
  8.5 1.2 copy-start.7
  9.7 1.2 copy-start.8
